TPU v7x, 256 devices: a whole 4x4x8 slice. The times are simulated.
256 devices in a mesh: tower: 2 (over core), tile: 128 (over x, z, y).
Axes of the slice: x: 4, y: 4, z: 8, core: 2. Of those that a mesh axis runs over, the one named last changes fastest.
Arguments:
- embeddings: bfloat16 [2, 65536, 1024], P('tower', 'tile'), may hold values from -2 to 2
- loss_weights: bfloat16 [2, 65536], P('tower', 'tile'), may hold values from 0.25 to 2
- dataset_of_block: int32 [128], replicated, may hold values from 0 to 41, never falling along the last dimension, each value on 1 to 6 neighbouring positions
- logit_scale: float32 [42], replicated, may hold values from 4 to 16
Outputs:
- grads: float32 [2, 65536, 1024], P('tower', 'tile')
Inputs may be any that keep to these rules, and one draw needn't show every extreme that they name: `dataset_of_block`: never falls along the blocks; each dataset covers 1 to 6 consecutive blocks, and one covers exactly 6.
All inputs are finite; a program needn't handle non-finite values.
Results may differ from a plain program's by a relative error of at most 0.0028.
Values may be sent and summed in bfloat16 or wider, within the bound.
A program may use at most 128 MiB of HBM per device.

v0:
```python
import jax
import jax.numpy as jnp
from jax import lax
from jax.sharding import PartitionSpec as P

MOSTB = 6


def from_behind(block, axis, distance):
    devices = range(lax.axis_size(axis))
    route = [(i - distance, i) for i in devices if i - distance in devices]
    return lax.ppermute(block, axis, route)


def partner(x, axis, apart):
    return lax.ppermute(x, axis, [(i, i ^ 1 << apart) for i in range(lax.axis_size(axis))])


def pick_value(table, index):
    return jnp.sum(jnp.where(jnp.arange(table.shape[0]) == index, table, jnp.zeros_like(table)))


def scores_of(mine, other, temper):
    return temper * lax.dot_general(
        mine, other, (((1,), (1,)), ((), ())), preferred_element_type=jnp.float32
    )


def fold_lse(state, mine, other, temper, live):

    def fold_work(carry):
        top, total = carry
        grid = scores_of(mine, other, temper)
        peak = jnp.maximum(top, jnp.max(grid, axis=1))
        total = total * jnp.exp(top - peak) + jnp.sum(jnp.exp(grid - peak[:, None]), axis=1)
        return (peak, total, grid)

    def fold_rest(carry):
        return (carry[0], carry[1], jnp.zeros((mine.shape[0], other.shape[0]), jnp.float32))

    return lax.cond(live, fold_work, fold_rest, state)


def add_grad(total, grid, other, lse_m, weight_m, lse_o, weight_o, diagonal):
    mass = weight_m[:, None] * jnp.exp(grid - lse_m[:, None]) + weight_o[None, :] * jnp.exp(
        grid - lse_o[None, :]
    )
    if diagonal:
        rows_here = lax.broadcasted_iota(jnp.int32, mass.shape, 0)
        cols_here = lax.broadcasted_iota(jnp.int32, mass.shape, 1)
        mass = mass - jnp.where(
            rows_here == cols_here, (weight_m + weight_o)[:, None], jnp.zeros_like(mass)
        )
    return total + jnp.dot(mass.astype(jnp.bfloat16), other, preferred_element_type=jnp.float32)


def move_lower(block):
    return from_behind(block, "tile", 1)


def move_upper(block):
    return from_behind(block, "tile", -1)


def stats_down(stats):
    return from_behind(stats, "tile", 1)


def stats_up(stats):
    return from_behind(stats, "tile", -1)


def again_down(block):
    return from_behind(block, "tile", 1)


def again_up(block):
    return from_behind(block, "tile", -1)


def on_device(embeddings, loss_weights, dataset_of_block, logit_scale):
    mine = embeddings[0]
    weight_half = loss_weights[0]
    other, weight_other = partner((mine, weight_half), "tower", 0)
    weight_m = weight_half.astype(jnp.float32)
    weight_o = weight_other.astype(jnp.float32)
    place = lax.axis_index("tile")
    extent = lax.axis_size("tile")
    my_set = pick_value(dataset_of_block, place)
    temper = jnp.sum(
        jnp.where(
            jnp.arange(logit_scale.shape[0]) == my_set, logit_scale, jnp.zeros_like(logit_scale)
        )
    )
    reach = MOSTB - 1

    def is_live(offset):
        target = place + offset
        inside = (target >= 0) & (target < extent)
        return inside & (pick_value(dataset_of_block, jnp.clip(target, 0, extent - 1)) == my_set)

    offsets = [0]
    visited = [other]
    lower_block = other
    upper_block = other
    for step in range(1, reach + 1):
        lower_block = move_lower(lower_block)
        upper_block = move_upper(upper_block)
        offsets = offsets + [-step, step]
        visited = visited + [lower_block, upper_block]
    state = (
        jnp.full((mine.shape[0],), -jnp.inf, jnp.float32),
        jnp.zeros((mine.shape[0],), jnp.float32),
    )
    stored = []
    for offset, block in zip(offsets, visited):
        top, total, grid = fold_lse(state, mine, block, temper, is_live(offset))
        state = (top, total)
        stored = stored + [grid]
    lse_m = state[0] + jnp.log(state[1])
    lse_o = partner(lse_m, "tower", 0)
    stats_list = [(lse_o, weight_o)]
    stats_low = (lse_o, weight_o)
    stats_high = (lse_o, weight_o)
    for step in range(1, reach + 1):
        stats_low = stats_down(stats_low)
        stats_high = stats_up(stats_high)
        stats_list = stats_list + [stats_low, stats_high]
    blocks_again = [other]
    lower_again = other
    upper_again = other
    for step in range(1, reach + 1):
        lower_again = again_down(lower_again)
        upper_again = again_up(upper_again)
        blocks_again = blocks_again + [lower_again, upper_again]
    total_grad = jnp.zeros(mine.shape, jnp.float32)
    for number, offset in enumerate(offsets):
        block = blocks_again[number]
        lse_cols, weight_cols = stats_list[number]
        saved = stored[number]
        diagonal = offset == 0

        def body_work(
            carry,
            block=block,
            lse_cols=lse_cols,
            weight_cols=weight_cols,
            saved=saved,
            diagonal=diagonal,
        ):
            grid = scores_of(mine, block, temper)
            return add_grad(carry, grid, block, lse_m, weight_m, lse_cols, weight_cols, diagonal)

        def body_rest(carry):
            return carry

        total_grad = lax.cond(is_live(offset), body_work, body_rest, total_grad)
    return (temper * total_grad)[None]


def solution(mesh):
    in_specs = (P("tower", "tile", None), P("tower", "tile"), P(), P())
    out_specs = P("tower", "tile", None)
    return jax.shard_map(
        on_device, mesh=mesh, in_specs=in_specs, out_specs=out_specs, check_vma=False
    )
```

profile of v0, /device:TPU:6, one launch (start us, length us, event | category | flops | bytes accessed | tf_op | source)
XLA Modules:
  0.0 293.7 jit_solution(462004998056994236)
XLA Ops:
  0.0 2.9 collective-permute-done
  2.9 3.5 %collective-permute-start.1 = (bf16[512,1024]{1,0:T(8,128)(2,1)S(1)}, bf16[512,1024]{1,0:T(8,128)(2,1)S(1)}, u32[]{:S(2)}, u32[]{:S(2)}) collective-permute-start(bf16[512,1024]{1,0:T(8,128)(2,1)S(1)} %collective-permute-done), channel_id=1, source_target_pairs={{0,1},{1,2},{2,3},{3,4},{4,5},{5,6},{6,7},{7,8},{8,9},{9,10},{10,1... | collective-permute-start | bytes 3145736 | tf_op jit(solution)/shard_map/ppermute | solution.py:12
  6.4 8.9 %collective-permute-start.2 = (bf16[512,1024]{1,0:T(8,128)(2,1)S(1)}, bf16[512,1024]{1,0:T(8,128)(2,1)S(1)}, u32[]{:S(2)}, u32[]{:S(2)}) collective-permute-start(bf16[512,1024]{1,0:T(8,128)(2,1)S(1)} %collective-permute-done), channel_id=1, source_target_pairs={{1,0},{2,1},{3,2},{4,3},{5,4},{6,5},{7,6},{8,7},{9,8},{10,9},{11,1... | collective-permute-start | bytes 3145736 | tf_op jit(solution)/shard_map/ppermute | solution.py:12
  15.3 21.5 %collective-permute-done.1 = bf16[512,1024]{1,0:T(8,128)(2,1)S(1)} collective-permute-done((bf16[512,1024]{1,0:T(8,128)(2,1)S(1)}, bf16[512,1024]{1,0:T(8,128)(2,1)S(1)}, u32[]{:S(2)}, u32[]{:S(2)}) %collective-permute-start.1) | collective-permute-done | bytes 1048608 | tf_op jit(solution)/shard_map/ppermute | solution.py:12
  36.8 1.9 collective-permute-start.3
  38.7 8.1 %collective-permute-start.4 = (bf16[512,1024]{1,0:T(8,128)(2,1)S(1)}, bf16[512,1024]{1,0:T(8,128)(2,1)S(1)}, u32[]{:S(2)}, u32[]{:S(2)}) collective-permute-start(bf16[512,1024]{1,0:T(8,128)(2,1)S(1)} %collective-permute-done.2), channel_id=1, source_target_pairs={{1,0},{2,1},{3,2},{4,3},{5,4},{6,5},{7,6},{8,7},{9,8},{10,9},{11,1... | collective-permute-start | bytes 3145736 | tf_op jit(solution)/shard_map/ppermute | solution.py:12
  46.9 20.7 %collective-permute-done.3 = bf16[512,1024]{1,0:T(8,128)(2,1)S(1)} collective-permute-done((bf16[512,1024]{1,0:T(8,128)(2,1)S(1)}, bf16[512,1024]{1,0:T(8,128)(2,1)S(1)}, u32[]{:S(2)}, u32[]{:S(2)}) %collective-permute-start.3) | collective-permute-done | bytes 1048608 | tf_op jit(solution)/shard_map/ppermute | solution.py:12
  67.6 1.9 collective-permute-start.5
  69.5 8.1 %collective-permute-start.6 = (bf16[512,1024]{1,0:T(8,128)(2,1)S(1)}, bf16[512,1024]{1,0:T(8,128)(2,1)S(1)}, u32[]{:S(2)}, u32[]{:S(2)}) collective-permute-start(bf16[512,1024]{1,0:T(8,128)(2,1)S(1)} %collective-permute-done.4), channel_id=1, source_target_pairs={{1,0},{2,1},{3,2},{4,3},{5,4},{6,5},{7,6},{8,7},{9,8},{10,9},{11,1... | collective-permute-start | bytes 3145736 | tf_op jit(solution)/shard_map/ppermute | solution.py:12
  77.7 19.8 %collective-permute-done.5 = bf16[512,1024]{1,0:T(8,128)(2,1)S(1)} collective-permute-done((bf16[512,1024]{1,0:T(8,128)(2,1)S(1)}, bf16[512,1024]{1,0:T(8,128)(2,1)S(1)}, u32[]{:S(2)}, u32[]{:S(2)}) %collective-permute-start.5) | collective-permute-done | bytes 1048608 | tf_op jit(solution)/shard_map/ppermute | solution.py:12
  97.5 1.9 collective-permute-start.7
  99.4 8.1 %collective-permute-start.8 = (bf16[512,1024]{1,0:T(8,128)(2,1)S(1)}, bf16[512,1024]{1,0:T(8,128)(2,1)}, u32[]{:S(2)}, u32[]{:S(2)}) collective-permute-start(bf16[512,1024]{1,0:T(8,128)(2,1)S(1)} %collective-permute-done.6), channel_id=1, source_target_pairs={{1,0},{2,1},{3,2},{4,3},{5,4},{6,5},{7,6},{8,7},{9,8},{10,9},{11,1... | collective-permute-start | bytes 3145736 | tf_op jit(solution)/shard_map/ppermute | solution.py:12
  107.6 19.0 %collective-permute-done.7 = bf16[512,1024]{1,0:T(8,128)(2,1)} collective-permute-done((bf16[512,1024]{1,0:T(8,128)(2,1)S(1)}, bf16[512,1024]{1,0:T(8,128)(2,1)}, u32[]{:S(2)}, u32[]{:S(2)}) %collective-permute-start.7) | collective-permute-done | bytes 1048608 | tf_op jit(solution)/shard_map/ppermute | solution.py:12
  126.6 1.9 collective-permute-start.9
  128.5 8.1 %collective-permute-start.10 = (bf16[512,1024]{1,0:T(8,128)(2,1)}, bf16[512,1024]{1,0:T(8,128)(2,1)S(1)}, u32[]{:S(2)}, u32[]{:S(2)}) collective-permute-start(bf16[512,1024]{1,0:T(8,128)(2,1)} %collective-permute-done.8), channel_id=1, source_target_pairs={{1,0},{2,1},{3,2},{4,3},{5,4},{6,5},{7,6},{8,7},{9,8},{10,9},{11,1... | collective-permute-start | bytes 3145736 | tf_op jit(solution)/shard_map/ppermute | solution.py:12
  136.7 1.5 fusion.71
  152.2 1.9 fusion.60
  154.1 5.1 %conditional.22 = (f32[512]{0:T(512)}, f32[512]{0:T(512)S(1)}) conditional(s32[]{:T(128)} %convert_element_type.93, () %tuple.150, (f32[]{:T(128)}, bf16[512,1024]{1,0:T(8,128)(2,1)}, bf16[512,1024]{1,0:T(8,128)(2,1)}) %tuple.296), branch_computations={%region_13.14_spmd, %region_14.17_spmd} | conditional | flops 537920000 | bytes 4206612 | solution.py:41
  154.1 3.5 %fusion.72 = (f32[512]{0:T(512)}, f32[512,512]{0,1:T(8,128)S(1)}) fusion(bf16[512,1024]{1,0:T(8,128)(2,1)} %get-tuple-element.379, bf16[512,1024]{1,0:T(8,128)(2,1)} %get-tuple-element.380, f32[]{:T(128)} %get-tuple-element.378), kind=kOutput, calls=%fused_computation.153 | convolution fusion | flops 537394688 | bytes 3147780 | tf_op jit(solution)/shard_map/cond/branch_1_fun/dot_general | solution.py:24
  157.6 0.9 exponential_reduce_fusion
  159.2 5.1 %conditional.23 = ((f32[512]{0:T(512)}, f32[512]{0:T(512)S(1)})) conditional(s32[]{:T(128)} %convert_element_type.92, (f32[512]{0:T(512)}, f32[512]{0:T(512)S(1)}) %conditional.22, (f32[]{:T(128)}, bf16[512,1024]{1,0:T(8,128)(2,1)}, bf16[512,1024]{1,0:T(8,128)(2,1)}, f32[512]{0:T(512)}, f32[512]{0:T(512)S(1)}) %tuple.294), branch_computations={%region_17.18_spmd, %region_18.21_spmd} | conditional | flops 537920512 | bytes 4220956 | solution.py:41
  159.2 2.9 fusion.73
  164.3 5.1 %conditional.24 = ((f32[512]{0:T(512)}, f32[512]{0:T(512)S(1)})) conditional(s32[]{:T(128)} %convert_element_type.91, (f32[512]{0:T(512)}, f32[512]{0:T(512)S(1)}) %get-tuple-element.645, (f32[]{:T(128)}, bf16[512,1024]{1,0:T(8,128)(2,1)}, bf16[512,1024]{1,0:T(8,128)(2,1)}, f32[512]{0:T(512)}, f32[512]{0:T(512)S(1)}) %tuple.292), branch_computations={%region_21.22_spmd, %region_22.25_spmd} | conditional | flops 537920512 | bytes 4220956 | solution.py:41
  164.3 2.9 fusion.74
  169.4 5.1 %conditional.25 = ((f32[512]{0:T(512)}, f32[512]{0:T(512)S(1)})) conditional(s32[]{:T(128)} %convert_element_type.90, (f32[512]{0:T(512)}, f32[512]{0:T(512)S(1)}) %get-tuple-element.646, (f32[]{:T(128)}, bf16[512,1024]{1,0:T(8,128)(2,1)}, bf16[512,1024]{1,0:T(8,128)(2,1)}, f32[512]{0:T(512)}, f32[512]{0:T(512)S(1)}) %tuple.290), branch_computations={%region_25.26_spmd, %region_26.0_spmd} | conditional | flops 537920512 | bytes 4220956 | solution.py:41
  169.4 2.9 fusion.75
  174.5 5.1 %conditional.26 = ((f32[512]{0:T(512)}, f32[512]{0:T(512)S(1)})) conditional(s32[]{:T(128)} %convert_element_type.89, (f32[512]{0:T(512)}, f32[512]{0:T(512)S(1)}) %get-tuple-element.647, (f32[]{:T(128)}, bf16[512,1024]{1,0:T(8,128)(2,1)}, bf16[512,1024]{1,0:T(8,128)(2,1)}, f32[512]{0:T(512)}, f32[512]{0:T(512)S(1)}) %tuple.288), branch_computations={%region_29.30_spmd, %region_30.0_spmd} | conditional | flops 537920512 | bytes 4220956 | solution.py:41
  174.5 2.9 fusion.76
  179.6 4.8 %conditional.28 = ((f32[512]{0:T(512)}, f32[512]{0:T(512)S(1)})) conditional(s32[]{:T(128)} %convert_element_type.87, (f32[512]{0:T(512)}, f32[512]{0:T(512)S(1)}) %get-tuple-element.649, (f32[]{:T(128)}, bf16[512,1024]{1,0:T(8,128)(2,1)}, bf16[512,1024]{1,0:T(8,128)(2,1)S(1)}, f32[512]{0:T(512)}, f32[512]{0:T(512)S(1)}) %tuple.270), branch_computations={%region_37.38_spmd, %region_38.41_spmd} | conditional | flops 537920512 | bytes 4220956 | solution.py:41
  179.6 2.6 fusion.78
  185.9 0.8 collective-permute-done.11
  186.7 1.9 collective-permute-start.13
  188.7 1.9 collective-permute-start.14
  190.6 8.1 %collective-permute-start.15 = (f32[512]{0:T(512)S(1)}, f32[512]{0:T(512)S(1)}, u32[]{:S(2)}, u32[]{:S(2)}) collective-permute-start(f32[512]{0:T(512)S(1)} %convert_element_type.95), channel_id=1, source_target_pairs={{1,0},{2,1},{3,2},{4,3},{5,4},{6,5},{7,6},{8,7},{9,8},{10,9},{11,1... | collective-permute-start | bytes 6152 | tf_op jit(solution)/shard_map/ppermute | solution.py:12
  198.7 3.9 %collective-permute-start.16 = (f32[512]{0:T(512)S(1)}, f32[512]{0:T(512)S(1)}, u32[]{:S(2)}, u32[]{:S(2)}) collective-permute-start(f32[512]{0:T(512)S(1)} %collective-permute-done.12), channel_id=1, source_target_pairs={{1,0},{2,1},{3,2},{4,3},{5,4},{6,5},{7,6},{8,7},{9,8},{10,9},{11,1... | collective-permute-start | bytes 6152 | tf_op jit(solution)/shard_map/ppermute | solution.py:12
  202.7 1.9 collective-permute-start.17
  204.6 1.9 collective-permute-start.18
  206.6 8.1 %collective-permute-start.19 = (f32[512]{0:T(512)S(1)}, f32[512]{0:T(512)S(1)}, u32[]{:S(2)}, u32[]{:S(2)}) collective-permute-start(f32[512]{0:T(512)S(1)} %collective-permute-done.15), channel_id=1, source_target_pairs={{1,0},{2,1},{3,2},{4,3},{5,4},{6,5},{7,6},{8,7},{9,8},{10,9},{11,1... | collective-permute-start | bytes 6152 | tf_op jit(solution)/shard_map/ppermute | solution.py:12
  214.7 3.9 %collective-permute-start.20 = (f32[512]{0:T(512)S(1)}, f32[512]{0:T(512)S(1)}, u32[]{:S(2)}, u32[]{:S(2)}) collective-permute-start(f32[512]{0:T(512)S(1)} %collective-permute-done.16), channel_id=1, source_target_pairs={{1,0},{2,1},{3,2},{4,3},{5,4},{6,5},{7,6},{8,7},{9,8},{10,9},{11,1... | collective-permute-start | bytes 6152 | tf_op jit(solution)/shard_map/ppermute | solution.py:12
  218.7 1.9 collective-permute-start.21
  220.6 1.9 collective-permute-start.22
  222.5 8.1 %collective-permute-start.23 = (f32[512]{0:T(512)S(1)}, f32[512]{0:T(512)S(1)}, u32[]{:S(2)}, u32[]{:S(2)}) collective-permute-start(f32[512]{0:T(512)S(1)} %collective-permute-done.19), channel_id=1, source_target_pairs={{1,0},{2,1},{3,2},{4,3},{5,4},{6,5},{7,6},{8,7},{9,8},{10,9},{11,1... | collective-permute-start | bytes 6152 | tf_op jit(solution)/shard_map/ppermute | solution.py:12
  230.7 3.9 %collective-permute-start.24 = (f32[512]{0:T(512)S(1)}, f32[512]{0:T(512)S(1)}, u32[]{:S(2)}, u32[]{:S(2)}) collective-permute-start(f32[512]{0:T(512)S(1)} %collective-permute-done.20), channel_id=1, source_target_pairs={{1,0},{2,1},{3,2},{4,3},{5,4},{6,5},{7,6},{8,7},{9,8},{10,9},{11,1... | collective-permute-start | bytes 6152 | tf_op jit(solution)/shard_map/ppermute | solution.py:12
  234.6 1.9 collective-permute-start.25
  236.6 1.9 collective-permute-start.26
  238.5 8.1 %collective-permute-start.27 = (f32[512]{0:T(512)S(1)}, f32[512]{0:T(512)}, u32[]{:S(2)}, u32[]{:S(2)}) collective-permute-start(f32[512]{0:T(512)S(1)} %collective-permute-done.23), channel_id=1, source_target_pairs={{1,0},{2,1},{3,2},{4,3},{5,4},{6,5},{7,6},{8,7},{9,8},{10,9},{11,1... | collective-permute-start | bytes 6152 | tf_op jit(solution)/shard_map/ppermute | solution.py:12
  246.7 3.9 %collective-permute-start.28 = (f32[512]{0:T(512)S(1)}, f32[512]{0:T(512)}, u32[]{:S(2)}, u32[]{:S(2)}) collective-permute-start(f32[512]{0:T(512)S(1)} %collective-permute-done.24), channel_id=1, source_target_pairs={{1,0},{2,1},{3,2},{4,3},{5,4},{6,5},{7,6},{8,7},{9,8},{10,9},{11,1... | collective-permute-start | bytes 6152 | tf_op jit(solution)/shard_map/ppermute | solution.py:12
  250.6 1.9 collective-permute-start.29
  252.6 1.9 collective-permute-start.30
  254.5 8.1 %collective-permute-start.31 = (f32[512]{0:T(512)}, f32[512]{0:T(512)S(1)}, u32[]{:S(2)}, u32[]{:S(2)}) collective-permute-start(f32[512]{0:T(512)} %collective-permute-done.27), channel_id=1, source_target_pairs={{1,0},{2,1},{3,2},{4,3},{5,4},{6,5},{7,6},{8,7},{9,8},{10,9},{11,1... | collective-permute-start | bytes 6152 | tf_op jit(solution)/shard_map/ppermute | solution.py:12
  262.6 3.9 %collective-permute-start.32 = (f32[512]{0:T(512)}, f32[512]{0:T(512)S(1)}, u32[]{:S(2)}, u32[]{:S(2)}) collective-permute-start(f32[512]{0:T(512)} %collective-permute-done.28), channel_id=1, source_target_pairs={{1,0},{2,1},{3,2},{4,3},{5,4},{6,5},{7,6},{8,7},{9,8},{10,9},{11,1... | collective-permute-start | bytes 6152 | tf_op jit(solution)/shard_map/ppermute | solution.py:12
  266.6 4.0 %conditional.33 = (f32[512,1024]{1,0:T(8,128)S(1)}) conditional(s32[]{:T(128)} %convert_element_type.93, () %tuple.149, (f32[512]{0:T(512)S(1)}, f32[]{:T(128)}, bf16[512,1024]{1,0:T(8,128)(2,1)}, bf16[512,1024]{1,0:T(8,128)(2,1)}, f32[512]{0:T(512)S(1)}, /*index=5*/f32[512]{0:T(512)S(1)}, f32[512]{0:T(512)S(1)}) %tuple.297), branch_computations={%region_57.58_spmd, %region_58.59_spmd} | conditional | flops 1076363776 | bytes 4210700 | solution.py:157
  266.6 4.0 %fusion = f32[512,1024]{1,0:T(8,128)S(1)} fusion(bf16[512,1024]{1,0:T(8,128)(2,1)} %get-tuple-element.434, bf16[512,1024]{1,0:T(8,128)(2,1)} %get-tuple-element.433, f32[512]{0:T(512)S(1)} %add.110, f32[512]{0:T(512)S(1)} %get-tuple-element.437, f32[512]{0:T(512)S(1)} %get-tuple-element.436, f32[512]{0:T(512)S(1)} %get-tuple-element.435, ...), kind=kOutput, calls=%fused_computation.36 | convolution fusion | flops 1076363264 | bytes 4204548 | tf_op jit(solution)/shard_map/cond/branch_1_fun/dot_general | solution.py:54
  270.6 4.2 %conditional.34 = (f32[512,1024]{1,0:T(8,128)S(1)}) conditional(s32[]{:T(128)} %convert_element_type.92, f32[512,1024]{1,0:T(8,128)S(1)} %get-tuple-element.655, (f32[512]{0:T(512)S(1)}, f32[]{:T(128)}, bf16[512,1024]{1,0:T(8,128)(2,1)}, bf16[512,1024]{1,0:T(8,128)(2,1)}, f32[512]{0:T(512)S(1)}, /*index=5*/f32[512]{0:T(512)S(1)}, ...), branch_computations={%region_59.60_spmd, %region_60.61_spmd} | conditional | flops 1076101120 | bytes 6299660 | solution.py:157
  270.7 4.1 %convolution_add_fusion = f32[512,1024]{1,0:T(8,128)S(1)} fusion(f32[512,1024]{1,0:T(8,128)S(1)} %get-tuple-element.438, bf16[512,1024]{1,0:T(8,128)(2,1)} %get-tuple-element.442, bf16[512,1024]{1,0:T(8,128)(2,1)} %get-tuple-element.441, f32[512]{0:T(512)S(1)} %get-tuple-element.445, f32[512]{0:T(512)S(1)} %get-tuple-element.444, ...), kind=kOutput, calls=%fused_computation.45 | convolution fusion | flops 1076101120 | bytes 6299652 | tf_op jit(solution)/shard_map/cond/branch_1_fun/dot_general | solution.py:54
  274.8 4.1 %conditional.35 = (f32[512,1024]{1,0:T(8,128)S(1)}) conditional(s32[]{:T(128)} %convert_element_type.91, f32[512,1024]{1,0:T(8,128)S(1)} %get-tuple-element.656, (f32[512]{0:T(512)S(1)}, f32[]{:T(128)}, bf16[512,1024]{1,0:T(8,128)(2,1)}, bf16[512,1024]{1,0:T(8,128)(2,1)}, f32[512]{0:T(512)S(1)}, /*index=5*/f32[512]{0:T(512)S(1)}, ...), branch_computations={%region_61.62_spmd, %region_62.63_spmd} | conditional | flops 1076101120 | bytes 6299660 | solution.py:157
  274.8 4.1 %convolution_add_fusion.1 = f32[512,1024]{1,0:T(8,128)S(1)} fusion(f32[512,1024]{1,0:T(8,128)S(1)} %get-tuple-element.446, bf16[512,1024]{1,0:T(8,128)(2,1)} %get-tuple-element.450, bf16[512,1024]{1,0:T(8,128)(2,1)} %get-tuple-element.449, f32[512]{0:T(512)S(1)} %get-tuple-element.453, f32[512]{0:T(512)S(1)} %get-tuple-element.452, ...), kind=kOutput, calls=%fused_computation.53 | convolution fusion | flops 1076101120 | bytes 6299652 | tf_op jit(solution)/shard_map/cond/branch_1_fun/dot_general | solution.py:54
  278.9 4.1 %conditional.36 = (f32[512,1024]{1,0:T(8,128)S(1)}) conditional(s32[]{:T(128)} %convert_element_type.90, f32[512,1024]{1,0:T(8,128)S(1)} %get-tuple-element.657, (f32[512]{0:T(512)S(1)}, f32[]{:T(128)}, bf16[512,1024]{1,0:T(8,128)(2,1)}, bf16[512,1024]{1,0:T(8,128)(2,1)}, f32[512]{0:T(512)S(1)}, /*index=5*/f32[512]{0:T(512)S(1)}, ...), branch_computations={%region_63.64_spmd, %region_64.65_spmd} | conditional | flops 1076101120 | bytes 6299660 | solution.py:157
  278.9 4.1 %convolution_add_fusion.2 = f32[512,1024]{1,0:T(8,128)S(1)} fusion(f32[512,1024]{1,0:T(8,128)S(1)} %get-tuple-element.454, bf16[512,1024]{1,0:T(8,128)(2,1)} %get-tuple-element.458, bf16[512,1024]{1,0:T(8,128)(2,1)} %get-tuple-element.457, f32[512]{0:T(512)S(1)} %get-tuple-element.461, f32[512]{0:T(512)S(1)} %get-tuple-element.460, ...), kind=kOutput, calls=%fused_computation.61 | convolution fusion | flops 1076101120 | bytes 6299652 | tf_op jit(solution)/shard_map/cond/branch_1_fun/dot_general | solution.py:54
  283.0 4.1 %conditional.37 = (f32[512,1024]{1,0:T(8,128)S(1)}) conditional(s32[]{:T(128)} %convert_element_type.89, f32[512,1024]{1,0:T(8,128)S(1)} %get-tuple-element.658, (f32[512]{0:T(512)S(1)}, f32[]{:T(128)}, bf16[512,1024]{1,0:T(8,128)(2,1)}, bf16[512,1024]{1,0:T(8,128)(2,1)}, f32[512]{0:T(512)S(1)}, /*index=5*/f32[512]{0:T(512)S(1)}, ...), branch_computations={%region_65.66_spmd, %region_66.67_spmd} | conditional | flops 1076101120 | bytes 6299660 | solution.py:157
  283.0 4.1 %convolution_add_fusion.3 = f32[512,1024]{1,0:T(8,128)S(1)} fusion(f32[512,1024]{1,0:T(8,128)S(1)} %get-tuple-element.462, bf16[512,1024]{1,0:T(8,128)(2,1)} %get-tuple-element.466, bf16[512,1024]{1,0:T(8,128)(2,1)} %get-tuple-element.465, f32[512]{0:T(512)S(1)} %get-tuple-element.469, f32[512]{0:T(512)S(1)} %get-tuple-element.468, ...), kind=kOutput, calls=%fused_computation.69 | convolution fusion | flops 1076101120 | bytes 6299652 | tf_op jit(solution)/shard_map/cond/branch_1_fun/dot_general | solution.py:54
  287.1 4.3 %conditional.39 = (f32[512,1024]{1,0:T(8,128)S(1)}) conditional(s32[]{:T(128)} %convert_element_type.87, f32[512,1024]{1,0:T(8,128)S(1)} %get-tuple-element.660, (f32[512]{0:T(512)S(1)}, f32[]{:T(128)}, bf16[512,1024]{1,0:T(8,128)(2,1)}, bf16[512,1024]{1,0:T(8,128)(2,1)}, f32[512]{0:T(512)S(1)}, /*index=5*/f32[512]{0:T(512)S(1)}, ...), branch_computations={%region_69.70_spmd, %region_70.71_spmd} | conditional | flops 1076101120 | bytes 6299660 | solution.py:157
  287.4 4.1 %convolution_add_fusion.5 = f32[512,1024]{1,0:T(8,128)S(1)} fusion(f32[512,1024]{1,0:T(8,128)S(1)} %get-tuple-element.478, bf16[512,1024]{1,0:T(8,128)(2,1)} %get-tuple-element.482, bf16[512,1024]{1,0:T(8,128)(2,1)} %get-tuple-element.481, f32[512]{0:T(512)S(1)} %get-tuple-element.485, f32[512]{0:T(512)S(1)} %get-tuple-element.484, ...), kind=kOutput, calls=%fused_computation.85 | convolution fusion | flops 1076101120 | bytes 6299652 | tf_op jit(solution)/shard_map/cond/branch_1_fun/dot_general | solution.py:54
  291.6 2.1 multiply_bitcast_fusion
  (82 shorter events, 13.2 us)
Async XLA Ops:
  0.0 2.9 collective-permute-start
  2.9 35.8 %copy-start.7 = (bf16[512,1024]{1,0:T(8,128)(2,1)}, bf16[512,1024]{1,0:T(8,128)(2,1)S(1)}, u32[]{:S(2)}) copy-start(bf16[512,1024]{1,0:T(8,128)(2,1)S(1)} %collective-permute-done) | copy-start | bytes 3145732
  2.9 33.9 %collective-permute-start.1 = (bf16[512,1024]{1,0:T(8,128)(2,1)S(1)}, bf16[512,1024]{1,0:T(8,128)(2,1)S(1)}, u32[]{:S(2)}, u32[]{:S(2)}) collective-permute-start(bf16[512,1024]{1,0:T(8,128)(2,1)S(1)} %collective-permute-done), channel_id=1, source_target_pairs={{0,1},{1,2},{2,3},{3,4},{4,5},{5,6},{6,7},{7,8},{8,9},{9,10},{10,1... | collective-permute-start | bytes 3145736 | tf_op jit(solution)/shard_map/ppermute | solution.py:12
  6.4 32.4 %collective-permute-start.2 = (bf16[512,1024]{1,0:T(8,128)(2,1)S(1)}, bf16[512,1024]{1,0:T(8,128)(2,1)S(1)}, u32[]{:S(2)}, u32[]{:S(2)}) collective-permute-start(bf16[512,1024]{1,0:T(8,128)(2,1)S(1)} %collective-permute-done), channel_id=1, source_target_pairs={{1,0},{2,1},{3,2},{4,3},{5,4},{6,5},{7,6},{8,7},{9,8},{10,9},{11,1... | collective-permute-start | bytes 3145736 | tf_op jit(solution)/shard_map/ppermute | solution.py:12
  36.8 99.9 %copy-start.6 = (bf16[512,1024]{1,0:T(8,128)(2,1)}, bf16[512,1024]{1,0:T(8,128)(2,1)S(1)}, u32[]{:S(2)}) copy-start(bf16[512,1024]{1,0:T(8,128)(2,1)S(1)} %collective-permute-done.1) | copy-start | bytes 3145732
  36.8 30.8 %collective-permute-start.3 = (bf16[512,1024]{1,0:T(8,128)(2,1)S(1)}, bf16[512,1024]{1,0:T(8,128)(2,1)S(1)}, u32[]{:S(2)}, u32[]{:S(2)}) collective-permute-start(bf16[512,1024]{1,0:T(8,128)(2,1)S(1)} %collective-permute-done.1), channel_id=1, source_target_pairs={{0,1},{1,2},{2,3},{3,4},{4,5},{5,6},{6,7},{7,8},{8,9},{9,10},{10,1... | collective-permute-start | bytes 3145736 | tf_op jit(solution)/shard_map/ppermute | solution.py:12
  38.7 97.9 %copy-start.5 = (bf16[512,1024]{1,0:T(8,128)(2,1)}, bf16[512,1024]{1,0:T(8,128)(2,1)S(1)}, u32[]{:S(2)}) copy-start(bf16[512,1024]{1,0:T(8,128)(2,1)S(1)} %collective-permute-done.2) | copy-start | bytes 3145732
  38.7 30.8 %collective-permute-start.4 = (bf16[512,1024]{1,0:T(8,128)(2,1)S(1)}, bf16[512,1024]{1,0:T(8,128)(2,1)S(1)}, u32[]{:S(2)}, u32[]{:S(2)}) collective-permute-start(bf16[512,1024]{1,0:T(8,128)(2,1)S(1)} %collective-permute-done.2), channel_id=1, source_target_pairs={{1,0},{2,1},{3,2},{4,3},{5,4},{6,5},{7,6},{8,7},{9,8},{10,9},{11,1... | collective-permute-start | bytes 3145736 | tf_op jit(solution)/shard_map/ppermute | solution.py:12
  67.6 60.9 %copy-start.4 = (bf16[512,1024]{1,0:T(8,128)(2,1)}, bf16[512,1024]{1,0:T(8,128)(2,1)S(1)}, u32[]{:S(2)}) copy-start(bf16[512,1024]{1,0:T(8,128)(2,1)S(1)} %collective-permute-done.3) | copy-start | bytes 3145732
  67.6 29.9 %collective-permute-start.5 = (bf16[512,1024]{1,0:T(8,128)(2,1)S(1)}, bf16[512,1024]{1,0:T(8,128)(2,1)S(1)}, u32[]{:S(2)}, u32[]{:S(2)}) collective-permute-start(bf16[512,1024]{1,0:T(8,128)(2,1)S(1)} %collective-permute-done.3), channel_id=1, source_target_pairs={{0,1},{1,2},{2,3},{3,4},{4,5},{5,6},{6,7},{7,8},{8,9},{9,10},{10,1... | collective-permute-start | bytes 3145736 | tf_op jit(solution)/shard_map/ppermute | solution.py:12
  69.5 59.0 %copy-start.3 = (bf16[512,1024]{1,0:T(8,128)(2,1)}, bf16[512,1024]{1,0:T(8,128)(2,1)S(1)}, u32[]{:S(2)}) copy-start(bf16[512,1024]{1,0:T(8,128)(2,1)S(1)} %collective-permute-done.4) | copy-start | bytes 3145732
  69.5 29.9 %collective-permute-start.6 = (bf16[512,1024]{1,0:T(8,128)(2,1)S(1)}, bf16[512,1024]{1,0:T(8,128)(2,1)S(1)}, u32[]{:S(2)}, u32[]{:S(2)}) collective-permute-start(bf16[512,1024]{1,0:T(8,128)(2,1)S(1)} %collective-permute-done.4), channel_id=1, source_target_pairs={{1,0},{2,1},{3,2},{4,3},{5,4},{6,5},{7,6},{8,7},{9,8},{10,9},{11,1... | collective-permute-start | bytes 3145736 | tf_op jit(solution)/shard_map/ppermute | solution.py:12
  97.5 82.1 %copy-start.2 = (bf16[512,1024]{1,0:T(8,128)(2,1)}, bf16[512,1024]{1,0:T(8,128)(2,1)S(1)}, u32[]{:S(2)}) copy-start(bf16[512,1024]{1,0:T(8,128)(2,1)S(1)} %collective-permute-done.5) | copy-start | bytes 3145732
  97.5 29.1 %collective-permute-start.7 = (bf16[512,1024]{1,0:T(8,128)(2,1)S(1)}, bf16[512,1024]{1,0:T(8,128)(2,1)}, u32[]{:S(2)}, u32[]{:S(2)}) collective-permute-start(bf16[512,1024]{1,0:T(8,128)(2,1)S(1)} %collective-permute-done.5), channel_id=1, source_target_pairs={{0,1},{1,2},{2,3},{3,4},{4,5},{5,6},{6,7},{7,8},{8,9},{9,10},{10,1... | collective-permute-start | bytes 3145736 | tf_op jit(solution)/shard_map/ppermute | solution.py:12
  99.4 80.2 %copy-start.1 = (bf16[512,1024]{1,0:T(8,128)(2,1)}, bf16[512,1024]{1,0:T(8,128)(2,1)S(1)}, u32[]{:S(2)}) copy-start(bf16[512,1024]{1,0:T(8,128)(2,1)S(1)} %collective-permute-done.6) | copy-start | bytes 3145732
  99.4 29.1 %collective-permute-start.8 = (bf16[512,1024]{1,0:T(8,128)(2,1)S(1)}, bf16[512,1024]{1,0:T(8,128)(2,1)}, u32[]{:S(2)}, u32[]{:S(2)}) collective-permute-start(bf16[512,1024]{1,0:T(8,128)(2,1)S(1)} %collective-permute-done.6), channel_id=1, source_target_pairs={{1,0},{2,1},{3,2},{4,3},{5,4},{6,5},{7,6},{8,7},{9,8},{10,9},{11,1... | collective-permute-start | bytes 3145736 | tf_op jit(solution)/shard_map/ppermute | solution.py:12
  126.6 57.8 %collective-permute-start.9 = (bf16[512,1024]{1,0:T(8,128)(2,1)}, bf16[512,1024]{1,0:T(8,128)(2,1)}, u32[]{:S(2)}, u32[]{:S(2)}) collective-permute-start(bf16[512,1024]{1,0:T(8,128)(2,1)} %collective-permute-done.7), channel_id=1, source_target_pairs={{0,1},{1,2},{2,3},{3,4},{4,5},{5,6},{6,7},{7,8},{8,9},{9,10},{10,1... | collective-permute-start | bytes 3145736 | tf_op jit(solution)/shard_map/ppermute | solution.py:12
  128.5 55.9 %collective-permute-start.10 = (bf16[512,1024]{1,0:T(8,128)(2,1)}, bf16[512,1024]{1,0:T(8,128)(2,1)S(1)}, u32[]{:S(2)}, u32[]{:S(2)}) collective-permute-start(bf16[512,1024]{1,0:T(8,128)(2,1)} %collective-permute-done.8), channel_id=1, source_target_pairs={{1,0},{2,1},{3,2},{4,3},{5,4},{6,5},{7,6},{8,7},{9,8},{10,9},{11,1... | collective-permute-start | bytes 3145736 | tf_op jit(solution)/shard_map/ppermute | solution.py:12
  184.4 0.9 copy-start
  185.3 3.4 %collective-permute-start.12 = (f32[512]{0:T(512)S(1)}, f32[512]{0:T(512)S(1)}, u32[]{:S(2)}, u32[]{:S(2)}) collective-permute-start(f32[512]{0:T(512)S(1)} %log_add_fusion), channel_id=1, source_target_pairs={{0,128},{128,0},{1,129},{129,1},{2,130},{130,2},{3,131},{131,3},{4... | collective-permute-start | bytes 6152 | tf_op jit(solution)/shard_map/ppermute | solution.py:16
  185.3 1.4 collective-permute-start.11
  186.7 15.9 %collective-permute-start.13 = (f32[512]{0:T(512)S(1)}, f32[512]{0:T(512)S(1)}, u32[]{:S(2)}, u32[]{:S(2)}) collective-permute-start(f32[512]{0:T(512)S(1)} %convert_element_type.95), channel_id=1, source_target_pairs={{0,1},{1,2},{2,3},{3,4},{4,5},{5,6},{6,7},{7,8},{8,9},{9,10},{10,1... | collective-permute-start | bytes 6152 | tf_op jit(solution)/shard_map/ppermute | solution.py:12
  188.7 15.9 %collective-permute-start.14 = (f32[512]{0:T(512)S(1)}, f32[512]{0:T(512)S(1)}, u32[]{:S(2)}, u32[]{:S(2)}) collective-permute-start(f32[512]{0:T(512)S(1)} %collective-permute-done.12), channel_id=1, source_target_pairs={{0,1},{1,2},{2,3},{3,4},{4,5},{5,6},{6,7},{7,8},{8,9},{9,10},{10,1... | collective-permute-start | bytes 6152 | tf_op jit(solution)/shard_map/ppermute | solution.py:12
  190.6 16.0 %collective-permute-start.15 = (f32[512]{0:T(512)S(1)}, f32[512]{0:T(512)S(1)}, u32[]{:S(2)}, u32[]{:S(2)}) collective-permute-start(f32[512]{0:T(512)S(1)} %convert_element_type.95), channel_id=1, source_target_pairs={{1,0},{2,1},{3,2},{4,3},{5,4},{6,5},{7,6},{8,7},{9,8},{10,9},{11,1... | collective-permute-start | bytes 6152 | tf_op jit(solution)/shard_map/ppermute | solution.py:12
  198.7 16.0 %collective-permute-start.16 = (f32[512]{0:T(512)S(1)}, f32[512]{0:T(512)S(1)}, u32[]{:S(2)}, u32[]{:S(2)}) collective-permute-start(f32[512]{0:T(512)S(1)} %collective-permute-done.12), channel_id=1, source_target_pairs={{1,0},{2,1},{3,2},{4,3},{5,4},{6,5},{7,6},{8,7},{9,8},{10,9},{11,1... | collective-permute-start | bytes 6152 | tf_op jit(solution)/shard_map/ppermute | solution.py:12
  202.7 16.0 %collective-permute-start.17 = (f32[512]{0:T(512)S(1)}, f32[512]{0:T(512)S(1)}, u32[]{:S(2)}, u32[]{:S(2)}) collective-permute-start(f32[512]{0:T(512)S(1)} %collective-permute-done.13), channel_id=1, source_target_pairs={{0,1},{1,2},{2,3},{3,4},{4,5},{5,6},{6,7},{7,8},{8,9},{9,10},{10,1... | collective-permute-start | bytes 6152 | tf_op jit(solution)/shard_map/ppermute | solution.py:12
  204.6 16.0 %collective-permute-start.18 = (f32[512]{0:T(512)S(1)}, f32[512]{0:T(512)S(1)}, u32[]{:S(2)}, u32[]{:S(2)}) collective-permute-start(f32[512]{0:T(512)S(1)} %collective-permute-done.14), channel_id=1, source_target_pairs={{0,1},{1,2},{2,3},{3,4},{4,5},{5,6},{6,7},{7,8},{8,9},{9,10},{10,1... | collective-permute-start | bytes 6152 | tf_op jit(solution)/shard_map/ppermute | solution.py:12
  206.6 16.0 %collective-permute-start.19 = (f32[512]{0:T(512)S(1)}, f32[512]{0:T(512)S(1)}, u32[]{:S(2)}, u32[]{:S(2)}) collective-permute-start(f32[512]{0:T(512)S(1)} %collective-permute-done.15), channel_id=1, source_target_pairs={{1,0},{2,1},{3,2},{4,3},{5,4},{6,5},{7,6},{8,7},{9,8},{10,9},{11,1... | collective-permute-start | bytes 6152 | tf_op jit(solution)/shard_map/ppermute | solution.py:12
  214.7 16.0 %collective-permute-start.20 = (f32[512]{0:T(512)S(1)}, f32[512]{0:T(512)S(1)}, u32[]{:S(2)}, u32[]{:S(2)}) collective-permute-start(f32[512]{0:T(512)S(1)} %collective-permute-done.16), channel_id=1, source_target_pairs={{1,0},{2,1},{3,2},{4,3},{5,4},{6,5},{7,6},{8,7},{9,8},{10,9},{11,1... | collective-permute-start | bytes 6152 | tf_op jit(solution)/shard_map/ppermute | solution.py:12
  218.7 16.0 %collective-permute-start.21 = (f32[512]{0:T(512)S(1)}, f32[512]{0:T(512)S(1)}, u32[]{:S(2)}, u32[]{:S(2)}) collective-permute-start(f32[512]{0:T(512)S(1)} %collective-permute-done.17), channel_id=1, source_target_pairs={{0,1},{1,2},{2,3},{3,4},{4,5},{5,6},{6,7},{7,8},{8,9},{9,10},{10,1... | collective-permute-start | bytes 6152 | tf_op jit(solution)/shard_map/ppermute | solution.py:12
  220.6 16.0 %collective-permute-start.22 = (f32[512]{0:T(512)S(1)}, f32[512]{0:T(512)S(1)}, u32[]{:S(2)}, u32[]{:S(2)}) collective-permute-start(f32[512]{0:T(512)S(1)} %collective-permute-done.18), channel_id=1, source_target_pairs={{0,1},{1,2},{2,3},{3,4},{4,5},{5,6},{6,7},{7,8},{8,9},{9,10},{10,1... | collective-permute-start | bytes 6152 | tf_op jit(solution)/shard_map/ppermute | solution.py:12
  222.5 16.0 %collective-permute-start.23 = (f32[512]{0:T(512)S(1)}, f32[512]{0:T(512)S(1)}, u32[]{:S(2)}, u32[]{:S(2)}) collective-permute-start(f32[512]{0:T(512)S(1)} %collective-permute-done.19), channel_id=1, source_target_pairs={{1,0},{2,1},{3,2},{4,3},{5,4},{6,5},{7,6},{8,7},{9,8},{10,9},{11,1... | collective-permute-start | bytes 6152 | tf_op jit(solution)/shard_map/ppermute | solution.py:12
  230.7 16.0 %collective-permute-start.24 = (f32[512]{0:T(512)S(1)}, f32[512]{0:T(512)S(1)}, u32[]{:S(2)}, u32[]{:S(2)}) collective-permute-start(f32[512]{0:T(512)S(1)} %collective-permute-done.20), channel_id=1, source_target_pairs={{1,0},{2,1},{3,2},{4,3},{5,4},{6,5},{7,6},{8,7},{9,8},{10,9},{11,1... | collective-permute-start | bytes 6152 | tf_op jit(solution)/shard_map/ppermute | solution.py:12
  234.6 16.0 %collective-permute-start.25 = (f32[512]{0:T(512)S(1)}, f32[512]{0:T(512)}, u32[]{:S(2)}, u32[]{:S(2)}) collective-permute-start(f32[512]{0:T(512)S(1)} %collective-permute-done.21), channel_id=1, source_target_pairs={{0,1},{1,2},{2,3},{3,4},{4,5},{5,6},{6,7},{7,8},{8,9},{9,10},{10,1... | collective-permute-start | bytes 6152 | tf_op jit(solution)/shard_map/ppermute | solution.py:12
  236.6 16.0 %collective-permute-start.26 = (f32[512]{0:T(512)S(1)}, f32[512]{0:T(512)}, u32[]{:S(2)}, u32[]{:S(2)}) collective-permute-start(f32[512]{0:T(512)S(1)} %collective-permute-done.22), channel_id=1, source_target_pairs={{0,1},{1,2},{2,3},{3,4},{4,5},{5,6},{6,7},{7,8},{8,9},{9,10},{10,1... | collective-permute-start | bytes 6152 | tf_op jit(solution)/shard_map/ppermute | solution.py:12
  238.5 16.0 %collective-permute-start.27 = (f32[512]{0:T(512)S(1)}, f32[512]{0:T(512)}, u32[]{:S(2)}, u32[]{:S(2)}) collective-permute-start(f32[512]{0:T(512)S(1)} %collective-permute-done.23), channel_id=1, source_target_pairs={{1,0},{2,1},{3,2},{4,3},{5,4},{6,5},{7,6},{8,7},{9,8},{10,9},{11,1... | collective-permute-start | bytes 6152 | tf_op jit(solution)/shard_map/ppermute | solution.py:12
  246.7 16.0 %collective-permute-start.28 = (f32[512]{0:T(512)S(1)}, f32[512]{0:T(512)}, u32[]{:S(2)}, u32[]{:S(2)}) collective-permute-start(f32[512]{0:T(512)S(1)} %collective-permute-done.24), channel_id=1, source_target_pairs={{1,0},{2,1},{3,2},{4,3},{5,4},{6,5},{7,6},{8,7},{9,8},{10,9},{11,1... | collective-permute-start | bytes 6152 | tf_op jit(solution)/shard_map/ppermute | solution.py:12
  250.6 40.9 %collective-permute-start.29 = (f32[512]{0:T(512)}, f32[512]{0:T(512)S(1)}, u32[]{:S(2)}, u32[]{:S(2)}) collective-permute-start(f32[512]{0:T(512)} %collective-permute-done.25), channel_id=1, source_target_pairs={{0,1},{1,2},{2,3},{3,4},{4,5},{5,6},{6,7},{7,8},{8,9},{9,10},{10,1... | collective-permute-start | bytes 6152 | tf_op jit(solution)/shard_map/ppermute | solution.py:12
  252.6 39.0 %collective-permute-start.30 = (f32[512]{0:T(512)}, f32[512]{0:T(512)S(1)}, u32[]{:S(2)}, u32[]{:S(2)}) collective-permute-start(f32[512]{0:T(512)} %collective-permute-done.26), channel_id=1, source_target_pairs={{0,1},{1,2},{2,3},{3,4},{4,5},{5,6},{6,7},{7,8},{8,9},{9,10},{10,1... | collective-permute-start | bytes 6152 | tf_op jit(solution)/shard_map/ppermute | solution.py:12
  254.5 37.0 %collective-permute-start.31 = (f32[512]{0:T(512)}, f32[512]{0:T(512)S(1)}, u32[]{:S(2)}, u32[]{:S(2)}) collective-permute-start(f32[512]{0:T(512)} %collective-permute-done.27), channel_id=1, source_target_pairs={{1,0},{2,1},{3,2},{4,3},{5,4},{6,5},{7,6},{8,7},{9,8},{10,9},{11,1... | collective-permute-start | bytes 6152 | tf_op jit(solution)/shard_map/ppermute | solution.py:12
  262.6 28.9 %collective-permute-start.32 = (f32[512]{0:T(512)}, f32[512]{0:T(512)S(1)}, u32[]{:S(2)}, u32[]{:S(2)}) collective-permute-start(f32[512]{0:T(512)} %collective-permute-done.28), channel_id=1, source_target_pairs={{1,0},{2,1},{3,2},{4,3},{5,4},{6,5},{7,6},{8,7},{9,8},{10,9},{11,1... | collective-permute-start | bytes 6152 | tf_op jit(solution)/shard_map/ppermute | solution.py:12
where the time goes:
time: 296 us; the launch traced here: 294 us
  starting transfers between devices  133 us (45%)
  waiting for transfers between devices  84.8 us (29%)
  matrix products  42.3 us (14%)
  other arithmetic  15.7 us (5%)
  between operations  14.6 us (5%)
  local copies, waits for them, and re-layouts  3.03 us (1%)
    ppermute x30, starting transfers between devices, from_behind(): return lax.ppermute(block, axis, route)  132 us
    ppermute x30, waiting for transfers between devices, from_behind(): return lax.ppermute(block, axis, route)  81.1 us
    dot_general x6, matrix products, add_grad(): jnp.dot(mass.astype(jnp.bfloat16), other, preferred_element_type=jnp.floa...  24.5 us
    dot_general x6, matrix products, scores_of(): lax.dot_general(mine, other, (((1,), (1,)), ((), ())), preferred_element_...  17.8 us
  transfers between devices with their start and end apart: 33, of which 6 were waited for; matrix products, arithmetic and copies ran while one was open for 20% of the time, Pallas kernels for 0%

commit v1 on v0

v1 whole, which is shorter than its diff:
```python
import jax
import jax.numpy as jnp
from jax import lax
from jax.experimental import pallas as pl
from jax.experimental.pallas import tpu as pltpu
from jax.sharding import PartitionSpec as P


MESH = pl.DeviceIdType.MESH
F32, BF16 = jnp.float32, jnp.bfloat16
BLK, D = 512, 1024
HALF = BLK // 2
COLS, LINES = 4, 32
NEG = -1e30
LOG2E = 1.4426950408889634
CH = 16

UNITS = 13


def kernel(ds_ref, scale_ref, x_ref, wt_ref, out_ref, held, score, mass, wts,
           row_m, row_l, col_m, col_l, lp, li, lf, lcol, mp, mi, mf,
           ya, yo, yi, zs, zr, zm, zo, zi, ends, edge,
           send, recv, s_in, s_mid, r_mid, s_out, r_out):
    t = lax.axis_index("tower")
    tile = lax.axis_index("tile")
    line, y = tile // COLS, tile % COLS
    sgn = 1 - 2 * (y // 2)
    far_k = 3 - 2 * (y // 2)

    def at(core, down, right):
        return (core, ((line + down + LINES) % LINES) * COLS + (y + right) % COLS)

    def rcopy(src, dst, ss, rs, dev):
        return pltpu.make_async_remote_copy(
            src_ref=src, dst_ref=dst, send_sem=ss, recv_sem=rs, device_id=dev, device_id_type=MESH)

    mate = at(1 - t, 0, 0)

    def arrived(ref, sem):
        rcopy(ref, ref, sem, sem, mate).wait_recv()

    barrier = pltpu.get_barrier_semaphore()
    peers = [mate]
    for core in (0, 1):
        for k in (1, 2, 3):
            peers.append(at(core, 0, k))
        for dz in (1, -1, 2, -2):
            peers.append(at(core, dz, 0))
    for dev in peers:
        pl.semaphore_signal(barrier, inc=1, device_id=dev, device_id_type=MESH)
    pl.semaphore_wait(barrier, len(peers))

    pending = []

    def go(copy):
        copy.start()
        pending.append(copy)
        return copy

    for j in (0, 1, 2):
        for g in (0, 1):
            right = (1 - t) * (j + 1)
            down = t * (1, -1, -2 * sgn)[j]
            unit = (1 - t) * (3 - j) + t * (6 + 2 * j + g)
            go(rcopy(x_ref.at[0, pl.ds(HALF * g, HALF)], held.at[unit], s_in.at[2 * j + g], recv.at[unit],
                     at(g, down, right)))
    for g in (0, 1):
        unit = (1 - t) * (12 - 12 * g) + t * (4 + g)
        go(rcopy(x_ref.at[0, pl.ds(HALF * g, HALF)], held.at[unit], s_in.at[6 + g], recv.at[unit], mate))
        mine = (1 - t) * (12 * g) + t * (4 + g)
        held[mine] = x_ref[0, HALF * g:HALF * g + HALF, :]
    wts[t] = jnp.broadcast_to(wt_ref[...].astype(F32), (8, BLK))
    go(rcopy(wts.at[t], wts.at[t], s_in.at[8], recv.at[13], mate))

    def block_of(down, right):
        return ds_ref[((line + down + LINES) % LINES) * COLS + (y + right) % COLS]

    def factors(k, b):
        mine = block_of(0, k)
        down = (0, -1, 1, 2 * sgn)[b]
        live = mine == block_of(down, 0)
        temper = scale_ref[mine] * LOG2E
        return jnp.where(live, temper, 0.0), jnp.where(live, 0.0, NEG)

    col_m[...] = jnp.full(col_m.shape, NEG, F32)
    col_l[...] = jnp.zeros(col_l.shape, F32)

    def video(b):
        return held[pl.ds(4 + 2 * b, 2)].reshape(BLK, D)

    def fold(k, blocks, slot):
        mults = [factors(k, b) for b in blocks]
        for b in blocks:
            at_score = 12 if b == 3 else 4 * b + k
            score[at_score] = lax.dot_general(held[k], video(b), (((1,), (1,)), ((), ())),
                                              preferred_element_type=F32)
        where_ = [12 if b == 3 else 4 * b + k for b in blocks]

        def rows(c, tops):
            at_rows = pl.ds(pl.multiple_of(c * CH, CH), CH)
            parts, peaks = [], []
            for n, b in enumerate(blocks):
                s = score[where_[n], at_rows, :] * mults[n][0] + mults[n][1]
                score[where_[n], at_rows, :] = s
                peaks.append(jnp.maximum(tops[n], jnp.maximum(s[0:8], s[8:16])))
                parts.extend([s[:, 128 * q:128 * q + 128] for q in range(4)])
            top = parts[0]
            for part in parts[1:]:
                top = jnp.maximum(top, part)
            total = jnp.exp2(parts[0] - top)
            for part in parts[1:]:
                total = total + jnp.exp2(part - top)
            row_m[slot, at_rows, :] = top
            row_l[slot, at_rows, :] = total
            return tuple(peaks)

        old = [col_m[b] for b in blocks]
        new = lax.fori_loop(0, HALF // CH, rows, tuple(old))

        def columns(c, sums):
            at_rows = pl.ds(pl.multiple_of(c * CH, CH), CH)
            result = []
            for n, b in enumerate(blocks):
                s = score[where_[n], at_rows, :]
                result.append(sums[n] + jnp.exp2(s[0:8] - new[n]) + jnp.exp2(s[8:16] - new[n]))
            return tuple(result)

        begin = tuple(col_l[b] * jnp.exp2(old[n] - new[n]) for n, b in enumerate(blocks))
        sums = lax.fori_loop(0, HALF // CH, columns, begin)
        for n, b in enumerate(blocks):
            col_m[b] = new[n]
            col_l[b] = sums[n]

    def forward(j):
        unit = 6 + 2 * j + t
        arrived(held.at[unit], recv.at[unit])
        go(rcopy(held.at[unit], held.at[unit], s_in.at[9 + j], recv.at[unit], mate))

    for g in (0, 1):
        unit = t * (12 - 12 * g) + (1 - t) * (4 + g)
        arrived(held.at[unit], recv.at[unit])
    arrived(wts.at[1 - t], recv.at[13])
    forward(0)
    forward(1)
    for j in (0, 1):
        unit = 6 + 2 * j + 1 - t
        arrived(held.at[unit], recv.at[unit])

    def one_unit(i, carry):
        k = i ^ (i // 2)

        @pl.when(k > 0)
        def _():
            arrived(held.at[k], recv.at[k])

        fold(k, (0, 1, 2), k)
        return carry

    lax.fori_loop(0, 3, one_unit, 0)
    forward(2)
    one_unit(3, 0)
    unit = 6 + 4 + 1 - t
    arrived(held.at[unit], recv.at[unit])
    fold(far_k, (3,), 4)

    lane = lax.broadcasted_iota(jnp.int32, (HALF, 128), 1)

    def pack_rows(k, carry):
        m, l = row_m[k], row_l[k]
        far_m = jnp.where(k == far_k, row_m[4], NEG)
        both = jnp.maximum(m, far_m)
        l = l * jnp.exp2(m - both) + row_l[4] * jnp.exp2(far_m - both)
        top = jnp.max(both, axis=1, keepdims=True)
        total = jnp.sum(l * jnp.exp2(both - top), axis=1, keepdims=True)
        lp[k] = jnp.where(lane == 0, top, total).T[0:8, :]
        return carry

    lax.fori_loop(0, 4, pack_rows, 0)
    for k in (1, 2, 3):
        go(rcopy(lp.at[k], li.at[k - 1], s_mid.at[k - 1], r_mid.at[k - 1], at(t, 0, k)))
    sub = lax.broadcasted_iota(jnp.int32, (8, BLK), 0)

    def pack_columns(b, carry):
        m, l = col_m[b], col_l[b]
        top = jnp.max(m, axis=0, keepdims=True)
        total = jnp.sum(l * jnp.exp2(m - top), axis=0, keepdims=True)
        mp[b] = jnp.where(sub == 0, top, total)
        return carry

    lax.fori_loop(0, 4, pack_columns, 0)
    go(rcopy(mp.at[0], mi.at[0], s_mid.at[3], r_mid.at[3], mate))
    for j in (0, 1, 2):
        for g in (0, 1):
            go(rcopy(mp.at[j + 1], mi.at[1 + 2 * j + t], s_mid.at[4 + 2 * j + g], r_mid.at[4 + 2 * j + t],
                     at(g, (-1, 1, 2 * sgn)[j], 0)))

    def merge(parts):
        tops = [p[0:1, :] for p in parts]
        top = tops[0]
        for other in tops[1:]:
            top = jnp.maximum(top, other)
        total = parts[0][1:2, :] * jnp.exp2(tops[0] - top)
        for n in range(1, len(parts)):
            total = total + parts[n][1:2, :] * jnp.exp2(tops[n] - top)
        return top + jnp.log(total) * LOG2E

    for k in (1, 2, 3):
        arrived(li.at[k - 1], r_mid.at[k - 1])
    w_half = wts[0, :, pl.ds(pl.multiple_of(HALF * t, HALF), HALF)][0:1, :]
    rows_lse = merge([lp[0]] + [li[k] for k in range(3)]) - jnp.log(w_half) * LOG2E
    lf[0] = jnp.broadcast_to(rows_lse, (8, HALF))
    for k in (1, 2, 3):
        go(rcopy(lf.at[0], lf.at[4 - k], s_mid.at[10 + k - 1], r_mid.at[10 + 4 - k - 1], at(t, 0, k)))
    for n in range(7):
        arrived(mi.at[n], r_mid.at[3 + n])
    cols_lse = merge([mp[0]] + [mi[n] for n in range(7)]) - jnp.log(wts[1][0:1, :]) * LOG2E
    mf[0] = jnp.broadcast_to(cols_lse, (8, BLK))
    for j in (0, 1, 2):
        go(rcopy(mf.at[0], mf.at[j + 1], s_mid.at[13 + j], r_mid.at[13 + j], at(t, (1, -1, -2 * sgn)[j], 0)))
    for k in (1, 2, 3):
        arrived(lf.at[k], r_mid.at[10 + k - 1])

    def turn(k, carry):
        lcol[k] = jnp.broadcast_to(lf[k][0:1, :], (128, HALF)).T
        return carry

    lax.fori_loop(0, 4, turn, 0)
    for j in (0, 1, 2):
        arrived(mf.at[j + 1], r_mid.at[13 + j])

    def derive(k, blocks):
        cols = [mf[b] for b in blocks]

        def rows(c, carry):
            at_rows = pl.ds(pl.multiple_of(c * CH, CH), CH)
            lse = lcol[k, at_rows, :]
            lse = jnp.concatenate([lse] * 4, axis=1)
            for n, b in enumerate(blocks):
                index = 12 if b == 3 else 4 * b + k
                s = score[index, at_rows, :]
                lse_c = jnp.concatenate([cols[n], cols[n]], axis=0)
                g = jnp.exp2(s - lse) + jnp.exp2(s - lse_c)
                if b == 0:
                    r_id = lax.broadcasted_iota(jnp.int32, (CH, BLK), 0) + c * CH + HALF * t + BLK * k
                    c_id = lax.broadcasted_iota(jnp.int32, (CH, BLK), 1)
                    both = jnp.concatenate([wts[0] + wts[1]] * 2, axis=0)
                    g = g - jnp.where(r_id == c_id, both, 0.0)
                mass[index, at_rows, :] = g.astype(BF16)
            return carry

        lax.fori_loop(0, HALF // CH, rows, 0)

    derive(far_k, (3,))
    edge[...] = jnp.dot(mass[12], video(3), preferred_element_type=F32)

    def row_grad(k):
        derive(k, (0, 1, 2))
        total = jnp.where(k == far_k, edge[...], 0.0)
        for b in (0, 1, 2):
            total = total + jnp.dot(mass[4 * b + k], video(b), preferred_element_type=F32)
        return total

    def outward(i, carry):
        k = 2 + i - 3 * (i // 2)
        yo[k - 1] = row_grad(k).astype(BF16)
        rcopy(yo.at[k - 1], yi.at[k - 1], s_out.at[k - 1], r_out.at[k - 1], at(t, 0, k)).start()
        return carry

    lax.fori_loop(0, 3, outward, 0)
    derive(0, (0, 1, 2))

    def col_grad(b, half):
        cols = pl.ds(pl.multiple_of(HALF * half, HALF), HALF)
        if b == 3:
            return lax.dot_general(mass[12, :, cols], held[far_k], (((0,), (0,)), ((), ())),
                                   preferred_element_type=F32)
        g = mass[4 * b:4 * b + 4, :, cols].reshape(4 * HALF, HALF)
        a = held[0:4].reshape(4 * HALF, D)
        return lax.dot_general(g, a, (((0,), (0,)), ((), ())), preferred_element_type=F32)

    for b in (3, 1, 2, 0):
        zs[b] = col_grad(b, 1 - t)
        go(rcopy(zs.at[b], zr.at[b], s_out.at[3 + b], r_out.at[3 + b], mate))
        zm[b] = col_grad(b, t)
    for b in (3, 1, 2):
        arrived(zr.at[b], r_out.at[3 + b])
        zo[b - 1] = (zm[b] + zr[b]).astype(BF16)
        go(rcopy(zo.at[b - 1], zi.at[b - 1], s_out.at[6 + b], r_out.at[6 + b], at(t, (0, -1, 1, 2 * sgn)[b], 0)))
    ya[...] = jnp.where(0 == far_k, edge[...], 0.0)
    for b in (0, 1, 2):
        ya[...] += jnp.dot(mass[4 * b], video(b), preferred_element_type=F32)

    temper = scale_ref[block_of(0, 0)]
    arrived(zr.at[0], r_out.at[3])
    for j in range(3):
        arrived(zi.at[j], r_out.at[7 + j])
    for k in range(3):
        arrived(yi.at[k], r_out.at[k])

    def finish(c, carry):
        at_rows = pl.ds(pl.multiple_of(c * CH, CH), CH)
        ga = ya[at_rows, :]
        gv = zm[0, at_rows, :] + zr[0, at_rows, :]
        for n in range(3):
            ga = ga + yi[n, at_rows, :].astype(F32)
            gv = gv + zi[n, at_rows, :].astype(F32)
        ends[0, at_rows, :] = temper * ga
        ends[1, at_rows, :] = temper * gv
        return carry

    lax.fori_loop(0, HALF // CH, finish, 0)
    half_rows = pl.ds(pl.multiple_of(HALF * t, HALF), HALF)
    other_rows = pl.ds(pl.multiple_of(HALF * (1 - t), HALF), HALF)
    go(rcopy(ends.at[1 - t], out_ref.at[0, half_rows], s_out.at[10], r_out.at[10], mate))
    out_ref[0, half_rows, :] = ends[t]
    arrived(out_ref.at[0, other_rows], r_out.at[10])
    for copy in pending:
        copy.wait_send()
    for k in (1, 2, 3):
        rcopy(yo.at[k - 1], yi.at[k - 1], s_out.at[k - 1], r_out.at[k - 1], at(t, 0, k)).wait_send()


def on_device(embeddings, loss_weights, dataset_of_block, logit_scale):
    vmem = pl.BlockSpec(memory_space=pltpu.VMEM)
    smem = pl.BlockSpec(memory_space=pltpu.SMEM)
    dma = pltpu.SemaphoreType.DMA
    scratch = [
        pltpu.VMEM((UNITS, HALF, D), BF16),
        pltpu.VMEM((13, HALF, BLK), F32),
        pltpu.VMEM((13, HALF, BLK), BF16),
        pltpu.VMEM((2, 8, BLK), F32),
        pltpu.VMEM((5, HALF, 128), F32),
        pltpu.VMEM((5, HALF, 128), F32),
        pltpu.VMEM((4, 8, BLK), F32),
        pltpu.VMEM((4, 8, BLK), F32),
        pltpu.VMEM((4, 8, HALF), F32),
        pltpu.VMEM((3, 8, HALF), F32),
        pltpu.VMEM((4, 8, HALF), F32),
        pltpu.VMEM((4, HALF, 128), F32),
        pltpu.VMEM((4, 8, BLK), F32),
        pltpu.VMEM((7, 8, BLK), F32),
        pltpu.VMEM((4, 8, BLK), F32),
        pltpu.VMEM((HALF, D), F32),
        pltpu.VMEM((3, HALF, D), BF16),
        pltpu.VMEM((3, HALF, D), BF16),
        pltpu.VMEM((4, HALF, D), F32),
        pltpu.VMEM((4, HALF, D), F32),
        pltpu.VMEM((4, HALF, D), F32),
        pltpu.VMEM((3, HALF, D), BF16),
        pltpu.VMEM((3, HALF, D), BF16),
        pltpu.VMEM((2, HALF, D), F32),
        pltpu.VMEM((HALF, D), F32),
        dma((1,)), dma((14,)), dma((12,)), dma((16,)), dma((16,)), dma((11,)), dma((11,)),
    ]
    return pl.pallas_call(
        kernel,
        out_shape=jax.ShapeDtypeStruct((1, BLK, D), F32),
        in_specs=[smem, smem, vmem, vmem],
        out_specs=vmem,
        scratch_shapes=scratch,
        compiler_params=pltpu.CompilerParams(
            collective_id=0, has_side_effects=True, vmem_limit_bytes=56 * 2**20),
    )(dataset_of_block, logit_scale, embeddings, loss_weights)


def solution(mesh):
    in_specs = (P("tower", "tile", None), P("tower", "tile"), P(), P())
    return jax.shard_map(
        on_device, mesh=mesh, in_specs=in_specs, out_specs=P("tower", "tile", None), check_vma=False)
```

time: 296 us -> 119 us (0.40)
  the two profiles are of different devices: /device:TPU:6 before, /device:TPU:1 now
where the time goes in v1:
time: 119 us
  Pallas kernels  116 us (97%)
  local copies, waits for them, and re-layouts  3.16 us (3%)
    pallas_call x1, Pallas kernels, on_device(): pl.pallas_call(kernel, out_shape=jax.ShapeDtypeStruct((1, BLK, D), F32),...  116 us
    unnamed x1, local copies, waits for them, and re-layouts  3.16 us

profile of v1, /device:TPU:1, one launch (start us, length us, event | category | flops | bytes accessed | tf_op | source)
XLA Modules:
  0.0 118.8 jit_solution(9969257990510865361)
XLA Ops:
  0.0 115.6 %shard_map.46 = f32[1,512,1024]{2,1,0:T(8,128)} custom-call(s32[128]{0:T(128)} %ds_ref.1, f32[42]{0:T(128)} %scale_ref.1, bf16[1,512,1024]{2,1,0:T(8,128)(2,1)} %x_ref.1, bf16[1,512]{1,0:T(2,128)(2,1)} %wt_ref.1), custom_call_target="tpu_custom_call" | custom-call | tf_op jit(solution)/shard_map/pallas_call | solution.py:356
  115.6 3.2 %copy.6 = f32[1,512,1024]{2,1,0:T(8,128)} copy(f32[1,512,1024]{2,1,0:T(8,128)} %shard_map.46) | data formatting | bytes 4194304

commit v2 on v1

v2 whole, which is shorter than its diff:
```python
import jax
import jax.numpy as jnp
from jax import lax
from jax.experimental import pallas as pl
from jax.experimental.pallas import tpu as pltpu
from jax.sharding import PartitionSpec as P


MESH = pl.DeviceIdType.MESH
F32, BF16 = jnp.float32, jnp.bfloat16
BLK, D = 512, 1024
HALF, QUART = BLK // 2, BLK // 4
COLS, LINES = 4, 32
NEG = -1e30
LOG2E = 1.4426950408889634
CH = 16

UNITS = 12


def kernel(ds_ref, scale_ref, x_ref, wt_ref, out_ref, held, score, mass, wts,
           row_m, row_l, col_m, col_l, lp, li, lf, lcol, mp, mi, mf,
           ya, yp, yo, yi, yt, yr, xo, xi, zs, zr, zm, zo, zi, ends,
           s_in, r_in, s_held, r_held, s_mid, r_mid, s_out, r_out):
    t = lax.axis_index("tower")
    tile = lax.axis_index("tile")
    line, y = tile // COLS, tile % COLS
    sel = y // 2
    sgn = 1 - 2 * sel
    edge = y % 3 == 0
    edge_k = 3 - 2 * sel
    edge_b = 2 - sel

    def at(core, down, right):
        return (core, ((line + down + LINES) % LINES) * COLS + (y + right) % COLS)

    def rcopy(src, dst, ss, rs, dev):
        return pltpu.make_async_remote_copy(
            src_ref=src, dst_ref=dst, send_sem=ss, recv_sem=rs, device_id=dev, device_id_type=MESH)

    mate = at(1 - t, 0, 0)
    across = at(t, -sgn, edge_k)

    def arrived(ref, sem):
        rcopy(ref, ref, sem, sem, mate).wait_recv()

    barrier = pltpu.get_barrier_semaphore()
    peers = [mate, at(t, 0, 2)]
    for core in (0, 1):
        for k in (1, 3):
            peers.append(at(core, 0, k))
        for dz in (1, -1):
            peers.append(at(core, dz, 0))
    for dev in peers:
        pl.semaphore_signal(barrier, inc=1, device_id=dev, device_id_type=MESH)

    @pl.when(edge)
    def _():
        pl.semaphore_signal(barrier, inc=1, device_id=across, device_id_type=MESH)

    pl.semaphore_wait(barrier, len(peers) + edge.astype(jnp.int32))

    pending, edge_pending = [], []

    def go(copy):
        copy.start()
        pending.append(copy)

    def edge_go(copy):
        edge_pending.append(copy)

        @pl.when(edge)
        def _():
            copy.start()

    def drain():
        for copy in pending:
            copy.wait_send()

        @pl.when(edge)
        def _():
            for copy in edge_pending:
                copy.wait_send()

    def half(h):
        return pl.ds(QUART * h, QUART)

    for step in (0, 1):
        for way in (0, 1):
            h = step ^ way
            for g in (0, 1):
                sign = 1 - 2 * way
                unit = (1 - t) * (3 - 2 * way) + t * (6 + 2 * way + g)
                go(rcopy(x_ref.at[0, pl.ds(HALF * g + QUART * h, QUART)], held.at[unit, half(h)],
                         s_in.at[4 * step + 2 * way + g], r_held.at[unit, h], at(g, t * sign, (1 - t) * sign)))
    for g in (0, 1):
        unit = (1 - t) * (11 - 11 * g) + t * (4 + g)
        go(rcopy(x_ref.at[0, pl.ds(HALF * g, HALF)], held.at[unit], s_in.at[8 + g], r_held.at[unit, 0], mate))
        mine = (1 - t) * (11 * g) + t * (4 + g)
        held[mine] = x_ref[0, HALF * g:HALF * g + HALF, :]
    wts[t] = jnp.broadcast_to(wt_ref[...].astype(F32), (8, BLK))
    go(rcopy(wts.at[t], wts.at[t], s_in.at[10], r_in.at[0], mate))

    def block_of(down, right):
        return ds_ref[((line + down + LINES) % LINES) * COLS + (y + right) % COLS]

    def factors(mine, other):
        live = mine == other
        temper = scale_ref[mine] * LOG2E
        return jnp.where(live, temper, 0.0), jnp.where(live, 0.0, NEG)

    col_m[...] = jnp.full(col_m.shape, NEG, F32)
    col_l[...] = jnp.zeros(col_l.shape, F32)
    row_m[4] = jnp.full((HALF, 128), NEG, F32)
    row_l[4] = jnp.zeros((HALF, 128), F32)

    def video(b):
        return held[pl.ds(4 + 2 * b, 2)].reshape(BLK, D)

    def fold(unit, slot, blocks):
        for b, index, mult, off in blocks:
            score[index] = lax.dot_general(held[unit], video(b), (((1,), (1,)), ((), ())),
                                           preferred_element_type=F32)

        def rows(c, tops):
            at_rows = pl.ds(pl.multiple_of(c * CH, CH), CH)
            parts, peaks = [], []
            for n, (b, index, mult, off) in enumerate(blocks):
                s = score[index, at_rows, :] * mult + off
                score[index, at_rows, :] = s
                peaks.append(jnp.maximum(tops[n], jnp.maximum(s[0:8], s[8:16])))
                parts.extend([s[:, 128 * q:128 * q + 128] for q in range(4)])
            top = parts[0]
            for part in parts[1:]:
                top = jnp.maximum(top, part)
            total = jnp.exp2(parts[0] - top)
            for part in parts[1:]:
                total = total + jnp.exp2(part - top)
            row_m[slot, at_rows, :] = top
            row_l[slot, at_rows, :] = total
            return tuple(peaks)

        old = [col_m[b] for b, _, _, _ in blocks]
        new = lax.fori_loop(0, HALF // CH, rows, tuple(old))

        def columns(c, sums):
            at_rows = pl.ds(pl.multiple_of(c * CH, CH), CH)
            result = []
            for n, (b, index, mult, off) in enumerate(blocks):
                s = score[index, at_rows, :]
                result.append(sums[n] + jnp.exp2(s[0:8] - new[n]) + jnp.exp2(s[8:16] - new[n]))
            return tuple(result)

        begin = tuple(col_l[b] * jnp.exp2(old[n] - new[n]) for n, (b, _, _, _) in enumerate(blocks))
        sums = lax.fori_loop(0, HALF // CH, columns, begin)
        for n, (b, _, _, _) in enumerate(blocks):
            col_m[b] = new[n]
            col_l[b] = sums[n]

    def fold_unit(k):
        mine = block_of(0, k)
        fold(k, k, [(b, 4 * b + k) + factors(mine, block_of((0, -1, 1)[b], 0)) for b in (0, 1, 2)])

    for g in (0, 1):
        unit = t * (11 - 11 * g) + (1 - t) * (4 + g)
        arrived(held.at[unit], r_held.at[unit, 0])
    arrived(wts.at[1 - t], r_in.at[0])

    for unit, h, way in ((3, 0, 1), (1, 1, -1)):
        arrived(held.at[unit, half(h)], r_held.at[unit, h])
        go(rcopy(held.at[unit, half(h)], held.at[2, half(h)], s_held.at[h], r_held.at[2, h], at(t, 0, way)))
    for j in (0, 1):
        unit = 6 + 2 * j + t
        for h in (0, 1):
            arrived(held.at[unit, half(h)], r_held.at[unit, h])
        go(rcopy(held.at[unit], held.at[unit], s_held.at[2 + j], r_held.at[unit, 0], mate))
    for unit, h in ((3, 1), (1, 0)):
        arrived(held.at[unit, half(h)], r_held.at[unit, h])

    edge_go(rcopy(held.at[edge_k], held.at[10], s_held.at[4], r_held.at[10, 0], at(t, sgn, 0)))

    for j in (0, 1):
        unit = 6 + 2 * j + 1 - t
        arrived(held.at[unit], r_held.at[unit, 0])

    def one_unit(i, carry):
        k = i ^ (i // 2)

        @pl.when(k == 2)
        def _():
            for h in (0, 1):
                arrived(held.at[2, half(h)], r_held.at[2, h])

        fold_unit(k)
        return carry

    lax.fori_loop(0, 4, one_unit, 0)

    @pl.when(edge)
    def _():
        arrived(held.at[10], r_held.at[10, 0])
        fold(10, 4, [(edge_b, 12) + factors(block_of(-sgn, edge_k), block_of(sgn, 0))])

    sub = lax.broadcasted_iota(jnp.int32, (2, BLK), 0)

    def pack_columns(b, carry):
        m, l = col_m[b], col_l[b]
        top = jnp.max(m, axis=0, keepdims=True)
        total = jnp.sum(l * jnp.exp2(m - top), axis=0, keepdims=True)
        mp[b] = jnp.where(sub == 0, top, total)
        return carry

    lax.fori_loop(0, 3, pack_columns, 0)
    for j in (0, 1):
        for g in (0, 1):
            go(rcopy(mp.at[j + 1], mi.at[2 * j + t], s_mid.at[2 * j + g], r_mid.at[2 * j + t],
                     at(g, (-1, 1)[j], 0)))
    go(rcopy(mp.at[0], mi.at[4], s_mid.at[4], r_mid.at[4], mate))
    lane = lax.broadcasted_iota(jnp.int32, (HALF, 128), 1)

    def pack_rows(k, carry):
        m, l = row_m[k], row_l[k]
        top = jnp.max(m, axis=1, keepdims=True)
        total = jnp.sum(l * jnp.exp2(m - top), axis=1, keepdims=True)
        lp[k] = jnp.where(lane == 0, top, total).T[0:2, :]
        return carry

    lax.fori_loop(0, 5, pack_rows, 0)
    for k in (1, 2, 3):
        go(rcopy(lp.at[k], li.at[k - 1], s_mid.at[4 + k], r_mid.at[4 + k], at(t, 0, k)))
    li[3] = jnp.where(sub[:, 0:HALF] == 0, NEG, 0.0)

    edge_go(rcopy(lp.at[4], li.at[4], s_mid.at[8], r_mid.at[8], across))

    def merge(parts):
        tops = [p[0:1, :] for p in parts]
        top = tops[0]
        for other in tops[1:]:
            top = jnp.maximum(top, other)
        total = parts[0][1:2, :] * jnp.exp2(tops[0] - top)
        for n in range(1, len(parts)):
            total = total + parts[n][1:2, :] * jnp.exp2(tops[n] - top)
        return top + jnp.log(total) * LOG2E

    for n in range(5):
        arrived(mi.at[n], r_mid.at[n])
    mf[0] = merge([mp[0]] + [mi[n] for n in range(5)]) - jnp.log(wts[1][0:1, :]) * LOG2E
    for j in (0, 1):
        go(rcopy(mf.at[0], mf.at[j + 1], s_mid.at[9 + j], r_mid.at[9 + j], at(t, (1, -1)[j], 0)))
    for k in (1, 2, 3):
        arrived(li.at[k - 1], r_mid.at[4 + k])

    @pl.when(edge)
    def _():
        arrived(li.at[4], r_mid.at[8])
        li[3] = li[4]

    w_half = wts[0, :, pl.ds(pl.multiple_of(HALF * t, HALF), HALF)][0:1, :]
    lf[0] = merge([lp[0]] + [li[n] for n in range(4)]) - jnp.log(w_half) * LOG2E
    for k in (1, 2, 3):
        go(rcopy(lf.at[0], lf.at[4 - k], s_mid.at[10 + k], r_mid.at[10 + 4 - k], at(t, 0, k)))

    edge_go(rcopy(lf.at[0], lf.at[4], s_mid.at[14], r_mid.at[14], across))

    for k in (1, 2, 3):
        arrived(lf.at[k], r_mid.at[10 + k])

    def turn(k):
        lcol[k] = jnp.broadcast_to(lf[k], (128, HALF)).T

    for k in range(4):
        turn(k)
    for j in (0, 1):
        arrived(mf.at[j + 1], r_mid.at[9 + j])

    def derive(slot, blocks):
        cols = [jnp.broadcast_to(mf[b], (CH, BLK)) for b, _ in blocks]

        def rows(c, carry):
            at_rows = pl.ds(pl.multiple_of(c * CH, CH), CH)
            lse = jnp.concatenate([lcol[slot, at_rows, :]] * 4, axis=1)
            for n, (b, index) in enumerate(blocks):
                s = score[index, at_rows, :]
                g = jnp.exp2(s - lse) + jnp.exp2(s - cols[n])
                if isinstance(b, int) and b == 0:
                    r_id = lax.broadcasted_iota(jnp.int32, (CH, BLK), 0) + c * CH + HALF * t + BLK * slot
                    c_id = lax.broadcasted_iota(jnp.int32, (CH, BLK), 1)
                    both = jnp.concatenate([wts[0] + wts[1]] * 2, axis=0)
                    g = g - jnp.where(r_id == c_id, both, 0.0)
                mass[index, at_rows, :] = g.astype(BF16)
            return carry

        lax.fori_loop(0, HALF // CH, rows, 0)

    def derive_unit(k):
        derive(k, [(b, 4 * b + k) for b in (0, 1, 2)])

    def row_grad(k):
        total = jnp.dot(mass[k], video(0), preferred_element_type=F32)
        for b in (1, 2):
            total = total + jnp.dot(mass[4 * b + k], video(b), preferred_element_type=F32)
        return total

    first = sel

    def quarter(h):
        return pl.ds(pl.multiple_of(QUART * h, QUART), QUART)

    @pl.when(edge)
    def _():
        arrived(lf.at[4], r_mid.at[14])
        turn(4)
        derive(4, [(edge_b, 12)])
        xo[...] = jnp.dot(mass[12], video(edge_b), preferred_element_type=F32).astype(BF16)

    for h in (first, 1 - first):
        edge_go(rcopy(xo.at[quarter(h)], xi.at[quarter(h)], s_out.at[h], r_out.at[h], at(t, -sgn, 0)))

    derive_unit(2)
    yt[...] = row_grad(2).astype(BF16)
    for h, way in ((0, 1), (1, -1)):
        go(rcopy(yt.at[half(h)], yr.at[h], s_out.at[2 + h], r_out.at[2 + h], at(t, 0, way)))

    def derive_rest(i, carry):
        derive_unit(i + i // 2)
        return carry

    lax.fori_loop(0, 3, derive_rest, 0)

    def col_grad(into, b, part):
        cols = pl.ds(pl.multiple_of(HALF * part, HALF), HALF)
        g = mass[4 * b:4 * b + 4, :, cols].reshape(4 * HALF, HALF)
        a = held[0:4].reshape(4 * HALF, D)
        into[b] = lax.dot_general(g, a, (((0,), (0,)), ((), ())), preferred_element_type=F32)
        if b > 0:
            @pl.when(edge & (edge_b == b))
            def _():
                into[b] += lax.dot_general(mass[12, :, cols], held[10], (((0,), (0,)), ((), ())),
                                           preferred_element_type=F32)

    for b in (1, 2):
        col_grad(zs, b, 1 - t)
        go(rcopy(zs.at[b], zr.at[b], s_out.at[4 + b], r_out.at[4 + b], mate))
    for b in (1, 2):
        col_grad(zm, b, t)
    for b in (1, 2):
        arrived(zr.at[b], r_out.at[4 + b])
        zo[b - 1] = (zm[b] + zr[b]).astype(BF16)
        go(rcopy(zo.at[b - 1], zi.at[b - 1], s_out.at[6 + b], r_out.at[6 + b], at(t, (0, -1, 1)[b], 0)))
    for n, k in ((0, 1), (1, 3)):
        yp[n] = row_grad(k)

    def add_edge(h):
        @pl.when(edge)
        def _():
            arrived(xi.at[quarter(h)], r_out.at[h])
            yp[1 - sel, quarter(h)] += xi[quarter(h)].astype(F32)

    def send_on(n, h):
        yo[n, half(h)] = yp[n, half(h)].astype(BF16)
        go(rcopy(yo.at[n, half(h)], yi.at[n, half(h)], s_out.at[9 + 2 * n + h], r_out.at[9 + 2 * n + h],
                 at(t, 0, 1 - 2 * n)))

    add_edge(first)
    send_on(0, 1)
    send_on(1, 0)
    add_edge(1 - first)
    for n in (0, 1):
        arrived(yr.at[n], r_out.at[2 + n])
        yp[n, half(n)] += yr[n].astype(F32)
        send_on(n, n)

    ya[...] = row_grad(0)
    col_grad(zs, 0, 1 - t)
    go(rcopy(zs.at[0], zr.at[0], s_out.at[4], r_out.at[4], mate))
    col_grad(zm, 0, t)

    temper = scale_ref[block_of(0, 0)]
    half_rows = pl.ds(pl.multiple_of(HALF * t, HALF), HALF)
    other_rows = pl.ds(pl.multiple_of(HALF * (1 - t), HALF), HALF)

    def finish(mode, value):
        def rows(c, carry):
            at_rows = pl.ds(pl.multiple_of(c * CH, CH), CH)
            ends[mode, at_rows, :] = temper * value(at_rows)
            return carry

        lax.fori_loop(0, HALF // CH, rows, 0)

        @pl.when(t == mode)
        def _():
            out_ref[0, half_rows, :] = ends[mode]

        @pl.when(t != mode)
        def _():
            rcopy(ends.at[mode], out_ref.at[0, half_rows], s_out.at[13], r_out.at[13], mate).start()

    for n in (0, 1):
        for h in (0, 1):
            arrived(yi.at[n, half(h)], r_out.at[9 + 2 * n + h])
    finish(0, lambda r: ya[r, :] + yi[0, r, :].astype(F32) + yi[1, r, :].astype(F32))
    arrived(zr.at[0], r_out.at[4])
    for j in (0, 1):
        arrived(zi.at[j], r_out.at[7 + j])
    finish(1, lambda r: zm[0, r, :] + zr[0, r, :] + zi[0, r, :].astype(F32) + zi[1, r, :].astype(F32))
    arrived(out_ref.at[0, other_rows], r_out.at[13])
    rcopy(ends.at[0], ends.at[0], s_out.at[13], r_out.at[13], mate).wait_send()
    drain()


def on_device(embeddings, loss_weights, dataset_of_block, logit_scale):
    vmem = pl.BlockSpec(memory_space=pltpu.VMEM)
    smem = pl.BlockSpec(memory_space=pltpu.SMEM)
    dma = pltpu.SemaphoreType.DMA
    scratch = [
        pltpu.VMEM((UNITS, HALF, D), BF16),
        pltpu.VMEM((13, HALF, BLK), F32),
        pltpu.VMEM((13, HALF, BLK), BF16),
        pltpu.VMEM((2, 8, BLK), F32),
        pltpu.VMEM((5, HALF, 128), F32),
        pltpu.VMEM((5, HALF, 128), F32),
        pltpu.VMEM((3, 8, BLK), F32),
        pltpu.VMEM((3, 8, BLK), F32),
        pltpu.VMEM((5, 2, HALF), F32),
        pltpu.VMEM((5, 2, HALF), F32),
        pltpu.VMEM((5, 1, HALF), F32),
        pltpu.VMEM((5, HALF, 128), F32),
        pltpu.VMEM((3, 2, BLK), F32),
        pltpu.VMEM((5, 2, BLK), F32),
        pltpu.VMEM((3, 1, BLK), F32),
        pltpu.VMEM((HALF, D), F32),
        pltpu.VMEM((2, HALF, D), F32),
        pltpu.VMEM((2, HALF, D), BF16),
        pltpu.VMEM((2, HALF, D), BF16),
        pltpu.VMEM((HALF, D), BF16),
        pltpu.VMEM((2, QUART, D), BF16),
        pltpu.VMEM((HALF, D), BF16),
        pltpu.VMEM((HALF, D), BF16),
        pltpu.VMEM((3, HALF, D), F32),
        pltpu.VMEM((3, HALF, D), F32),
        pltpu.VMEM((3, HALF, D), F32),
        pltpu.VMEM((2, HALF, D), BF16),
        pltpu.VMEM((2, HALF, D), BF16),
        pltpu.VMEM((2, HALF, D), F32),
        dma((11,)), dma((1,)), dma((5,)), dma((UNITS, 2)), dma((15,)), dma((15,)), dma((14,)), dma((14,)),
    ]
    return pl.pallas_call(
        kernel,
        out_shape=jax.ShapeDtypeStruct((1, BLK, D), F32),
        in_specs=[smem, smem, vmem, vmem],
        out_specs=vmem,
        scratch_shapes=scratch,
        compiler_params=pltpu.CompilerParams(
            collective_id=0, has_side_effects=True, vmem_limit_bytes=56 * 2**20),
    )(dataset_of_block, logit_scale, embeddings, loss_weights)


def solution(mesh):
    in_specs = (P("tower", "tile", None), P("tower", "tile"), P(), P())
    return jax.shard_map(
        on_device, mesh=mesh, in_specs=in_specs, out_specs=P("tower", "tile", None), check_vma=False)
```

time: 119 us -> 84.2 us (0.71)
  Pallas kernels: 116 us -> 80.9 us
    pallas_call x1, Pallas kernels: 116 us -> 80.9 us  [on_device(): pl.pallas_call(kernel, out_shape=jax.ShapeDtypeStruct((1, BLK, D), F32),...]
where the time goes in v2:
time: 84.2 us; the launch traced here: 84 us
  Pallas kernels  80.9 us (96%)
  local copies, waits for them, and re-layouts  3.16 us (4%)
    pallas_call x1, Pallas kernels, on_device(): pl.pallas_call(kernel, out_shape=jax.ShapeDtypeStruct((1, BLK, D), F32),...  80.9 us
    unnamed x1, local copies, waits for them, and re-layouts  3.16 us

profile of v2, /device:TPU:1, one launch (start us, length us, event | category | flops | bytes accessed | tf_op | source)
XLA Modules:
  0.0 84.0 jit_solution(15663228634493943724)
XLA Ops:
  0.0 80.9 %shard_map.46 = f32[1,512,1024]{2,1,0:T(8,128)} custom-call(s32[128]{0:T(128)} %ds_ref.1, f32[42]{0:T(128)} %scale_ref.1, bf16[1,512,1024]{2,1,0:T(8,128)(2,1)} %x_ref.1, bf16[1,512]{1,0:T(2,128)(2,1)} %wt_ref.1), custom_call_target="tpu_custom_call" | custom-call | tf_op jit(solution)/shard_map/pallas_call | solution.py:447
  80.9 3.2 %copy.6 = f32[1,512,1024]{2,1,0:T(8,128)} copy(f32[1,512,1024]{2,1,0:T(8,128)} %shard_map.46) | data formatting | bytes 4194304

commit v3 on v2

v3 whole, which is shorter than its diff:
```python
import jax
import jax.numpy as jnp
from jax import lax
from jax.experimental import pallas as pl
from jax.experimental.pallas import tpu as pltpu
from jax.sharding import PartitionSpec as P


MESH = pl.DeviceIdType.MESH
F32, BF16 = jnp.float32, jnp.bfloat16
BLK, D = 512, 1024
HALF, PART = BLK // 2, BLK // 8
COLS, LINES = 4, 32
NEG = -1e30
LOG2E = 1.4426950408889634
CH = 64

UNITS = 11


def kernel(ds_ref, scale_ref, x_ref, wt_ref, out_ref, held, score, mass, wts,
           row_m, row_l, col_m, col_l, lp, li, lf, lcol, mp, mi, mf,
           ya, yp, yo, yi, yt, yr, xs, xo, zf, zr, zo, zi, ends,
           s_in, r_in, s_held, r_held, s_mid, r_mid, s_out, r_out, s_y, r_y, s_z, r_z, s_home, s_away, r_away):
    t = lax.axis_index("tower")
    tile = lax.axis_index("tile")
    line, y = tile // COLS, tile % COLS
    sel = y // 2
    sgn = 1 - 2 * sel
    edge = y % 3 == 0
    edge_k = 3 - 2 * sel
    edge_u = 2 - sel
    edge_b = 2 - sel
    late_b = 1 + sel

    def at(core, down, right):
        return (core, ((line + down + LINES) % LINES) * COLS + (y + right) % COLS)

    def rcopy(src, dst, ss, rs, dev):
        return pltpu.make_async_remote_copy(
            src_ref=src, dst_ref=dst, send_sem=ss, recv_sem=rs, device_id=dev, device_id_type=MESH)

    mate = at(1 - t, 0, 0)
    across = at(t, -sgn, edge_k)

    def arrived(ref, sem):
        rcopy(ref, ref, sem, sem, mate).wait_recv()

    barrier = pltpu.get_barrier_semaphore()
    peers = [mate, at(t, 0, 2)]
    for core in (0, 1):
        for k in (1, 3):
            peers.append(at(core, 0, k))
        for dz in (1, -1):
            peers.append(at(core, dz, 0))
    for dev in peers:
        pl.semaphore_signal(barrier, inc=1, device_id=dev, device_id_type=MESH)

    @pl.when(edge)
    def _():
        pl.semaphore_signal(barrier, inc=1, device_id=across, device_id_type=MESH)

    waiting = []
    for g in (0, 1):
        own = (1 - t) * (10 * g) + t * (4 + g)
        waiting.append(pltpu.make_async_copy(x_ref.at[0, pl.ds(HALF * g, HALF)], held.at[own], s_in.at[19 + g]))
        waiting[-1].start()
    wts[t] = jnp.broadcast_to(wt_ref[...].astype(F32), (8, BLK))
    col_m[...] = jnp.full(col_m.shape, NEG, F32)
    col_l[...] = jnp.zeros(col_l.shape, F32)
    row_m[4] = jnp.full((HALF, 128), NEG, F32)
    row_l[4] = jnp.zeros((HALF, 128), F32)
    pl.semaphore_wait(barrier, len(peers) + edge.astype(jnp.int32))

    pending, edge_pending = [], []

    def go(copy):
        copy.start()
        pending.append(copy)

    def edge_go(copy):
        edge_pending.append(copy)

        @pl.when(edge)
        def _():
            copy.start()

    def drain():
        for copy in pending:
            copy.wait_send()
        for step in range(4):
            for way in (0, 1):
                @pl.when(jnp.logical_not(direct[4 * step + 2 * way][1]))
                def _():
                    for g in (0, 1):
                        direct[4 * step + 2 * way + g][0].wait_send()

        @pl.when(edge)
        def _():
            for copy in edge_pending:
                copy.wait_send()

    def half(h):
        return pl.ds(HALF // 2 * h, HALF // 2)

    def part(q):
        return pl.ds(PART * q if isinstance(q, int) else pl.multiple_of(PART * q, PART), PART)

    direct = []
    for step in range(4):
        for way in (0, 1):
            q = step if way == 0 else 3 - step
            held_back = edge & (sel == way) & (t == 1)
            for g in (0, 1):
                sign = 1 - 2 * way
                unit = (1 - t) * (2 - way) + t * (6 + 2 * way + g)
                copy = rcopy(x_ref.at[0, pl.ds(HALF * g + PART * q, PART)], held.at[unit, part(q)],
                             s_in.at[4 * step + 2 * way + g], r_held.at[unit, q], at(g, t * sign, (1 - t) * sign))
                direct.append((copy, held_back))

    for g in (0, 1):
        unit = (1 - t) * (10 - 10 * g) + t * (4 + g)
        go(rcopy(x_ref.at[0, pl.ds(HALF * g, HALF)], held.at[unit], s_in.at[16 + g], r_held.at[unit, 0], mate))
    go(rcopy(wts.at[t], wts.at[t], s_in.at[18], r_in.at[0], mate))
    for step in range(4):
        for way in (0, 1):
            @pl.when(jnp.logical_not(direct[4 * step + 2 * way][1]))
            def _():
                for g in (0, 1):
                    direct[4 * step + 2 * way + g][0].start()

    def block_of(down, right):
        return ds_ref[((line + down + LINES) % LINES) * COLS + (y + right) % COLS]

    def factors(mine, other):
        live = mine == other
        temper = scale_ref[mine] * LOG2E
        return jnp.where(live, temper, 0.0), jnp.where(live, 0.0, NEG)

    def video(b):
        return held[pl.ds(4 + 2 * b, 2)].reshape(BLK, D)

    def multiply(first, count, b, index):
        score[pl.ds(index, count)] = lax.dot_general(
            held[pl.ds(first, count)].reshape(count * HALF, D), video(b), (((1,), (1,)), ((), ())),
            preferred_element_type=F32).reshape(count, HALF, BLK)

    def fold(slot, blocks):
        def rows(c, tops):
            at_rows = pl.ds(pl.multiple_of(c * CH, CH), CH)
            parts, peaks = [], []
            for n, (b, index, mult, off) in enumerate(blocks):
                s = score[index, at_rows, :] * mult + off
                score[index, at_rows, :] = s
                peak = tops[n]
                for e in range(0, CH, 8):
                    peak = jnp.maximum(peak, s[e:e + 8])
                peaks.append(peak)
                parts.extend([s[:, 128 * q:128 * q + 128] for q in range(4)])
            top = parts[0]
            for part in parts[1:]:
                top = jnp.maximum(top, part)
            total = jnp.exp2(parts[0] - top)
            for part in parts[1:]:
                total = total + jnp.exp2(part - top)
            row_m[slot, at_rows, :] = top
            row_l[slot, at_rows, :] = total
            return tuple(peaks)

        old = [col_m[b] for b, _, _, _ in blocks]
        new = lax.fori_loop(0, HALF // CH, rows, tuple(old))

        def columns(c, sums):
            at_rows = pl.ds(pl.multiple_of(c * CH, CH), CH)
            result = []
            for n, (b, index, mult, off) in enumerate(blocks):
                s = score[index, at_rows, :]
                total = sums[n]
                for e in range(0, CH, 8):
                    total = total + jnp.exp2(s[e:e + 8] - new[n])
                result.append(total)
            return tuple(result)

        begin = tuple(col_l[b] * jnp.exp2(old[n] - new[n]) for n, (b, _, _, _) in enumerate(blocks))
        sums = lax.fori_loop(0, HALF // CH, columns, begin)
        for n, (b, _, _, _) in enumerate(blocks):
            col_m[b] = new[n]
            col_l[b] = sums[n]

    def tile_of(u, b):
        k = u ^ (u // 2)
        return (b, 4 * b + u) + factors(block_of(0, k), block_of((b == 2) * 1 - (b == 1) * 1, 0))

    for copy in waiting:
        copy.wait()
    for g in (0, 1):
        unit = t * (10 - 10 * g) + (1 - t) * (4 + g)
        arrived(held.at[unit], r_held.at[unit, 0])
    arrived(wts.at[1 - t], r_in.at[0])

    multiply(0, 1, 0, 0)
    fold(0, [tile_of(0, 0)])

    give = edge & (block_of(0, edge_k) == block_of(2 * sgn, 0))
    for step in range(4):
        for unit, q in ((2, step), (1, 3 - step)):
            arrived(held.at[unit, part(q)], r_held.at[unit, q])
        if step == 2:
            for unit, h, way in ((2, 0, 1), (1, 1, -1)):
                go(rcopy(held.at[unit, half(h)], held.at[3, half(h)], s_held.at[h], r_held.at[3, h], at(t, 0, way)))
        q = step + sel * (3 - 2 * step)

        @pl.when(edge)
        def _():
            xs[part(q)] = jnp.where(give, held[edge_u, part(q), :], held[4 + t, part(q), :])

        unit = 4 + 2 * late_b + t
        edge_go(rcopy(xs.at[part(q)], held.at[unit, part(q)], s_held.at[4 + step], r_held.at[unit, q], at(t, sgn, 0)))

    def share(b, sem):
        unit = 4 + 2 * b + t
        for step in range(4):
            q = step if sem < 12 else step + sel * (3 - 2 * step)
            arrived(held.at[unit, part(q)], r_held.at[unit, q])
            go(rcopy(held.at[unit, part(q)], held.at[unit, part(q)], s_held.at[sem + step], r_held.at[unit, q], mate))

    def shared(b):
        unit = 4 + 2 * b + 1 - t
        for q in range(4):
            arrived(held.at[unit, part(q)], r_held.at[unit, q])

    share(edge_b, 8)
    shared(edge_b)

    multiply(1, 2, 0, 1)
    multiply(0, 3, edge_b, 4 * edge_b)
    fold(5, [tile_of(0, edge_b)])

    def early(u, carry):
        fold(u, [tile_of(u, 0), tile_of(u, edge_b)])
        return carry

    lax.fori_loop(1, 3, early, 0)
    share(late_b, 12)

    lane = lax.broadcasted_iota(jnp.int32, (HALF, 128), 1)

    def unite(u, slot):
        m, other = row_m[u], row_m[slot]
        top = jnp.maximum(m, other)
        row_l[u] = row_l[u] * jnp.exp2(m - top) + row_l[slot] * jnp.exp2(other - top)
        row_m[u] = top

    def pack_rows(u):
        m, l = row_m[u], row_l[u]
        top = jnp.max(m, axis=1, keepdims=True)
        total = jnp.sum(l * jnp.exp2(m - top), axis=1, keepdims=True)
        lp[u] = jnp.where(lane == 0, top, total).T[0:2, :]

    def send_rows(u):
        k = u ^ (u // 2)
        go(rcopy(lp.at[u], li.at[k - 1], s_mid.at[4 + k], r_mid.at[4 + k], at(t, 0, k)))

    @pl.when(edge)
    def _():
        multiply(4 + 2 * late_b + t, 1, edge_b, 12)
        fold(4, [(edge_b, 12) + factors(block_of(-sgn, edge_k), block_of(sgn, 0))])
        pack_rows(4)

    edge_go(rcopy(lp.at[4], li.at[4], s_mid.at[8], r_mid.at[8], across))
    shared(late_b)
    multiply(0, 3, late_b, 4 * late_b)

    def late(u, carry):
        fold(6 + u, [tile_of(u, late_b)])
        return carry

    lax.fori_loop(0, 3, late, 0)

    for u, slot in ((1, 7), (2, 8)):
        unite(u, slot)
        pack_rows(u)
        send_rows(u)
    for h in (0, 1):
        arrived(held.at[3, half(h)], r_held.at[3, h])
    for b in (0, 1, 2):
        multiply(3, 1, b, 4 * b + 3)
    fold(3, [tile_of(3, b) for b in (0, 1, 2)])
    pack_rows(3)
    send_rows(3)
    sub = lax.broadcasted_iota(jnp.int32, (2, BLK), 0)

    def pack_columns(b, carry):
        m, l = col_m[b], col_l[b]
        top = jnp.max(m, axis=0, keepdims=True)
        total = jnp.sum(l * jnp.exp2(m - top), axis=0, keepdims=True)
        mp[b] = jnp.where(sub == 0, top, total)
        return carry

    lax.fori_loop(0, 3, pack_columns, 0)
    for j in (0, 1):
        for g in (0, 1):
            go(rcopy(mp.at[j + 1], mi.at[2 * j + t], s_mid.at[2 * j + g], r_mid.at[2 * j + t],
                     at(g, (-1, 1)[j], 0)))
    go(rcopy(mp.at[0], mi.at[4], s_mid.at[4], r_mid.at[4], mate))
    for slot in (5, 6):
        unite(0, slot)
    pack_rows(0)
    li[3] = jnp.where(sub[:, 0:HALF] == 0, NEG, 0.0)

    def merge(parts):
        tops = [p[0:1, :] for p in parts]
        top = tops[0]
        for other in tops[1:]:
            top = jnp.maximum(top, other)
        total = parts[0][1:2, :] * jnp.exp2(tops[0] - top)
        for n in range(1, len(parts)):
            total = total + parts[n][1:2, :] * jnp.exp2(tops[n] - top)
        return top + jnp.log(total) * LOG2E

    for n in range(5):
        arrived(mi.at[n], r_mid.at[n])
    mf[0] = merge([mp[0]] + [mi[n] for n in range(5)]) - jnp.log(wts[1][0:1, :]) * LOG2E
    for j in (0, 1):
        go(rcopy(mf.at[0], mf.at[j + 1], s_mid.at[9 + j], r_mid.at[9 + j], at(t, (1, -1)[j], 0)))
    for k in (1, 2, 3):
        arrived(li.at[k - 1], r_mid.at[4 + k])

    @pl.when(edge)
    def _():
        arrived(li.at[4], r_mid.at[8])
        li[3] = li[4]

    w_half = wts[0, :, pl.ds(pl.multiple_of(HALF * t, HALF), HALF)][0:1, :]
    lf[0] = merge([lp[0]] + [li[n] for n in range(4)]) - jnp.log(w_half) * LOG2E
    for k in (1, 2, 3):
        go(rcopy(lf.at[0], lf.at[(4 - k) ^ ((4 - k) // 2)], s_mid.at[10 + k], r_mid.at[10 + 4 - k], at(t, 0, k)))

    edge_go(rcopy(lf.at[0], lf.at[4], s_mid.at[14], r_mid.at[14], across))

    for k in (1, 2, 3):
        arrived(lf.at[k ^ (k // 2)], r_mid.at[10 + k])

    def turn(k):
        lcol[k] = jnp.broadcast_to(lf[k], (128, HALF)).T

    for k in range(4):
        turn(k)
    for j in (0, 1):
        arrived(mf.at[j + 1], r_mid.at[9 + j])

    def derive(slot, blocks, diagonal=False):
        cols = [jnp.broadcast_to(mf[b], (CH, BLK)) for b, _ in blocks]

        def rows(c, carry):
            at_rows = pl.ds(pl.multiple_of(c * CH, CH), CH)
            lse = jnp.concatenate([lcol[slot, at_rows, :]] * 4, axis=1)
            for n, (b, index) in enumerate(blocks):
                s = score[index, at_rows, :]
                g = jnp.exp2(s - lse) + jnp.exp2(s - cols[n])
                if diagonal:
                    r_id = lax.broadcasted_iota(jnp.int32, (CH, BLK), 0) + c * CH + HALF * t
                    c_id = lax.broadcasted_iota(jnp.int32, (CH, BLK), 1)
                    both = jnp.broadcast_to(wts[0][0:1, :] + wts[1][0:1, :], (CH, BLK))
                    g = g - jnp.where(r_id == c_id, both, 0.0)
                mass[index, at_rows, :] = g.astype(BF16)
            return carry

        lax.fori_loop(0, HALF // CH, rows, 0)

    def derive_units(first, last, blocks):
        def one(u, carry):
            derive(u, [(b, 4 * b + u) for b in blocks])
            return carry

        lax.fori_loop(first, last, one, 0)

    def row_grad(first, count):
        def term(b):
            return jnp.dot(mass[4 * b + first:4 * b + first + count].reshape(count * HALF, BLK), video(b),
                           preferred_element_type=F32)

        return term(0) + term(1) + term(2)

    mine = pl.ds(pl.multiple_of(HALF * t, HALF), HALF)
    others = pl.ds(pl.multiple_of(HALF * (1 - t), HALF), HALF)

    def col_grad(b, sem, far=False):
        for rows in (others, mine):
            g = mass[pl.ds(4 * b, 4), :, rows].reshape(4 * HALF, HALF)
            a = held[0:4].reshape(4 * HALF, D)
            zf[b, rows] = lax.dot_general(g, a, (((0,), (0,)), ((), ())), preferred_element_type=F32)
            if far:
                @pl.when(edge)
                def _():
                    zf[b, rows] += lax.dot_general(mass[12, :, rows], held[4 + 2 * late_b + t],
                                                   (((0,), (0,)), ((), ())), preferred_element_type=F32)
            if rows is others:
                go(rcopy(zf.at[b, others], zr.at[b], s_out.at[sem], r_out.at[sem], mate))

    @pl.when(edge)
    def _():
        arrived(lf.at[4], r_mid.at[14])
        turn(4)
        derive(4, [(edge_b, 12)])

    derive_units(0, 4, (late_b,))
    col_grad(late_b, 5)

    @pl.when(edge)
    def _():
        xo[...] = jnp.dot(mass[12], video(edge_b), preferred_element_type=F32)

    derive_units(3, 4, (0, edge_b))

    def send_lines(b, sem, base, down, order):
        arrived(zr.at[b], r_out.at[sem])
        zo[b - 1] = (zf[b, mine] + zr[b]).astype(BF16)
        for step in range(4):
            q = step + order * (3 - 2 * step)
            go(rcopy(zo.at[b - 1, part(q)], zi.at[b - 1, part(q)], s_z.at[base, q], r_z.at[b - 1, q],
                     at(t, down, 0)))

    @pl.when(edge)
    def _():
        zf[late_b, mine] += xo[...]

    send_lines(late_b, 5, 0, -sgn, sel)
    yt[...] = row_grad(3, 1).astype(BF16)
    for h, way in ((0, 1), (1, -1)):
        go(rcopy(yt.at[half(h)], yr.at[h], s_out.at[2 + h], r_out.at[2 + h], at(t, 0, way)))
    derive_units(0, 3, (edge_b,))
    col_grad(edge_b, 6, True)
    derive(0, [(0, 0)], True)
    derive_units(1, 3, (0,))
    yp[...] = row_grad(1, 2).reshape(2, HALF, D)
    send_lines(edge_b, 6, 1, sgn, 1 - sel)

    for step in range(4):
        q = step + sel * (3 - 2 * step)

        @pl.when(edge)
        def _():
            arrived(zi.at[sel, part(q)], r_z.at[sel, q])
            yp[1 - sel, part(q)] += jnp.where(give, zi[sel, part(q), :].astype(F32), 0.0)

        if step == 2:
            for n in (0, 1):
                arrived(yr.at[n], r_out.at[2 + n])
                yp[n, half(n)] += yr[n].astype(F32)
        for n, q in ((0, 3 - step), (1, step)):
            yo[n, part(q)] = yp[n, part(q)].astype(BF16)
            go(rcopy(yo.at[n, part(q)], yi.at[n, part(q)], s_y.at[n, q], r_y.at[n, q], at(t, 0, 1 - 2 * n)))

    col_grad(0, 4)
    ya[...] = row_grad(0, 1)

    temper = scale_ref[block_of(0, 0)]
    home, away = [], []
    for q in range(4):
        to = out_ref.at[0, pl.ds(pl.multiple_of(HALF * t + PART * q, PART), PART)]
        home.append(pltpu.make_async_copy(ends.at[t, part(q)], to, s_home.at[q]))
        away.append(rcopy(ends.at[1 - t, part(q)], to, s_away.at[q], r_away.at[q], mate))

    def finish(mode, q, value):
        ends[mode, part(q)] = temper * value

        @pl.when(t == mode)
        def _():
            home[q].start()

        @pl.when(t != mode)
        def _():
            away[q].start()

    arrived(zr.at[0], r_out.at[4])
    for q in (1, 2, 0, 3):
        rows = part(q)
        for n in (0, 1):
            arrived(yi.at[n, rows], r_y.at[n, q])
        finish(0, q, ya[rows, :] + yi[0, rows, :].astype(F32) + yi[1, rows, :].astype(F32))
        for j in (0, 1):
            @pl.when(jnp.logical_not(edge & (sel == j)))
            def _():
                arrived(zi.at[j, rows], r_z.at[j, q])

        mine_q = pl.ds(pl.multiple_of(HALF * t + PART * q, PART), PART)
        finish(1, q, (zf[0, mine_q, :] + zr[0, rows, :]
                      + jnp.where(give & (sel == 0), 0.0, zi[0, rows, :].astype(F32))
                      + jnp.where(give & (sel == 1), 0.0, zi[1, rows, :].astype(F32))))
    for q in range(4):
        home[q].wait()
        away[q].wait_send()
        to = out_ref.at[0, pl.ds(pl.multiple_of(HALF * (1 - t) + PART * q, PART), PART)]
        rcopy(to, to, s_away.at[q], r_away.at[q], mate).wait_recv()
    drain()


def on_device(embeddings, loss_weights, dataset_of_block, logit_scale):
    vmem = pl.BlockSpec(memory_space=pltpu.VMEM)
    smem = pl.BlockSpec(memory_space=pltpu.SMEM)
    hbm = pl.BlockSpec(memory_space=pl.ANY)
    dma = pltpu.SemaphoreType.DMA
    scratch = [
        pltpu.VMEM((UNITS, HALF, D), BF16),
        pltpu.VMEM((13, HALF, BLK), F32),
        pltpu.VMEM((13, HALF, BLK), BF16),
        pltpu.VMEM((2, 8, BLK), F32),
        pltpu.VMEM((9, HALF, 128), F32),
        pltpu.VMEM((9, HALF, 128), F32),
        pltpu.VMEM((3, 8, BLK), F32),
        pltpu.VMEM((3, 8, BLK), F32),
        pltpu.VMEM((5, 2, HALF), F32),
        pltpu.VMEM((5, 2, HALF), F32),
        pltpu.VMEM((5, 1, HALF), F32),
        pltpu.VMEM((5, HALF, 128), F32),
        pltpu.VMEM((3, 2, BLK), F32),
        pltpu.VMEM((5, 2, BLK), F32),
        pltpu.VMEM((3, 1, BLK), F32),
        pltpu.VMEM((HALF, D), F32),
        pltpu.VMEM((2, HALF, D), F32),
        pltpu.VMEM((2, HALF, D), BF16),
        pltpu.VMEM((2, HALF, D), BF16),
        pltpu.VMEM((HALF, D), BF16),
        pltpu.VMEM((2, HALF // 2, D), BF16),
        pltpu.VMEM((HALF, D), BF16),
        pltpu.VMEM((HALF, D), F32),
        pltpu.VMEM((3, BLK, D), F32),
        pltpu.VMEM((3, HALF, D), F32),
        pltpu.VMEM((2, HALF, D), BF16),
        pltpu.VMEM((2, HALF, D), BF16),
        pltpu.VMEM((2, HALF, D), F32),
        dma((21,)), dma((1,)), dma((16,)), dma((UNITS, 4)), dma((15,)), dma((15,)), dma((14,)), dma((14,)),
        dma((2, 4)), dma((2, 4)), dma((2, 4)), dma((2, 4)), dma((4,)), dma((4,)), dma((4,)),
    ]
    return pl.pallas_call(
        kernel,
        out_shape=jax.ShapeDtypeStruct((1, BLK, D), F32),
        in_specs=[smem, smem, hbm, vmem],
        out_specs=hbm,
        scratch_shapes=scratch,
        compiler_params=pltpu.CompilerParams(
            collective_id=0, has_side_effects=True, vmem_limit_bytes=56 * 2**20),
    )(dataset_of_block, logit_scale, embeddings, loss_weights)


def solution(mesh):
    in_specs = (P("tower", "tile", None), P("tower", "tile"), P(), P())
    return jax.shard_map(
        on_device, mesh=mesh, in_specs=in_specs, out_specs=P("tower", "tile", None), check_vma=False)
```

time: 84.2 us -> 78.8 us (0.936)
  Pallas kernels: 80.9 us -> 75.4 us
    pallas_call x1, Pallas kernels: 80.9 us -> 75.4 us  [on_device(): pl.pallas_call(kernel, out_shape=jax.ShapeDtypeStruct((1, BLK, D), F32),...]
where the time goes in v3:
time: 78.8 us; the launch traced here: 78.6 us
  Pallas kernels  75.4 us (96%)
  local copies, waits for them, and re-layouts  3.16 us (4%)
    pallas_call x1, Pallas kernels, on_device(): pl.pallas_call(kernel, out_shape=jax.ShapeDtypeStruct((1, BLK, D), F32),...  75.4 us
    unnamed x1, local copies, waits for them, and re-layouts  3.16 us

profile of v3, /device:TPU:1, one launch (start us, length us, event | category | flops | bytes accessed | tf_op | source)
XLA Modules:
  0.0 78.6 jit_solution(11719732672795947832)
XLA Ops:
  0.0 75.4 %shard_map.46 = f32[1,512,1024]{2,1,0:T(8,128)} custom-call(s32[128]{0:T(128)} %ds_ref.1, f32[42]{0:T(128)} %scale_ref.1, bf16[1,512,1024]{2,1,0:T(8,128)(2,1)} %x_ref.1, bf16[1,512]{1,0:T(2,128)(2,1)} %wt_ref.1), custom_call_target="tpu_custom_call" | custom-call | tf_op jit(solution)/shard_map/pallas_call | solution.py:536
  75.5 3.2 %copy.6 = f32[1,512,1024]{2,1,0:T(8,128)} copy(f32[1,512,1024]{2,1,0:T(8,128)} %shard_map.46) | data formatting | bytes 4194304

commit v4 on v3

--- a/solution.py
+++ b/solution.py
@@ -19,7 +19,7 @@
 
 
 def kernel(ds_ref, scale_ref, x_ref, wt_ref, out_ref, held, score, mass, wts,
-           row_m, row_l, col_m, col_l, lp, li, lf, lcol, mp, mi, mf,
+           row_m, row_l, col_m, col_l, lp, li, lx, lf, lcol, mp, m1, m2, m3, mf,
            ya, yp, yo, yi, yt, yr, xs, xo, zf, zr, zo, zi, ends,
            s_in, r_in, s_held, r_held, s_mid, r_mid, s_out, r_out, s_y, r_y, s_z, r_z, s_home, s_away, r_away):
     t = lax.axis_index("tower")
@@ -51,14 +51,17 @@
     for core in (0, 1):
         for k in (1, 3):
             peers.append(at(core, 0, k))
-        for dz in (1, -1):
+        for dz in (1, -1, 2, -2):
             peers.append(at(core, dz, 0))
+    peers.append(at(t, 1, COLS - y))
+    peers.append(at(t, -1, COLS - 1 - y))
     for dev in peers:
         pl.semaphore_signal(barrier, inc=1, device_id=dev, device_id_type=MESH)
 
     @pl.when(edge)
     def _():
-        pl.semaphore_signal(barrier, inc=1, device_id=across, device_id_type=MESH)
+        for c in range(COLS):
+            pl.semaphore_signal(barrier, inc=1, device_id=at(t, -sgn, c), device_id_type=MESH)
 
     waiting = []
     for g in (0, 1):
@@ -70,7 +73,7 @@
     col_l[...] = jnp.zeros(col_l.shape, F32)
     row_m[4] = jnp.full((HALF, 128), NEG, F32)
     row_l[4] = jnp.zeros((HALF, 128), F32)
-    pl.semaphore_wait(barrier, len(peers) + edge.astype(jnp.int32))
+    pl.semaphore_wait(barrier, len(peers) + COLS * edge.astype(jnp.int32))
 
     pending, edge_pending = [], []
 
@@ -197,6 +200,9 @@
         unit = t * (10 - 10 * g) + (1 - t) * (4 + g)
         arrived(held.at[unit], r_held.at[unit, 0])
     arrived(wts.at[1 - t], r_in.at[0])
+    log_w = jnp.log(wts[0, :, pl.ds(pl.multiple_of(HALF * t, HALF), HALF)][0:1, :]) * LOG2E
+    lp[2, 0:1, :] = log_w
+    mp[1, 2:3, :] = jnp.log(wts[1][0:1, :]) * LOG2E
 
     multiply(0, 1, 0, 0)
     fold(0, [tile_of(0, 0)])
@@ -255,11 +261,12 @@
         m, l = row_m[u], row_l[u]
         top = jnp.max(m, axis=1, keepdims=True)
         total = jnp.sum(l * jnp.exp2(m - top), axis=1, keepdims=True)
-        lp[u] = jnp.where(lane == 0, top, total).T[0:2, :]
-
-    def send_rows(u):
-        k = u ^ (u // 2)
-        go(rcopy(lp.at[u], li.at[k - 1], s_mid.at[4 + k], r_mid.at[4 + k], at(t, 0, k)))
+        turned = jnp.where(lane == 0, top, total).T
+        if u == 4:
+            lp[3, 0:2, :] = turned[0:2, :]
+        else:
+            lp[0, u:u + 1, :] = turned[0:1, :]
+            lp[1, u:u + 1, :] = turned[1:2, :]
 
     @pl.when(edge)
     def _():
@@ -267,7 +274,8 @@
         fold(4, [(edge_b, 12) + factors(block_of(-sgn, edge_k), block_of(sgn, 0))])
         pack_rows(4)
 
-    edge_go(rcopy(lp.at[4], li.at[4], s_mid.at[8], r_mid.at[8], across))
+    for c in range(COLS):
+        edge_go(rcopy(lp.at[3], lx.at[sel], s_mid.at[c], r_mid.at[sel], at(t, -sgn, c)))
     shared(late_b)
     multiply(0, 3, late_b, 4 * late_b)
 
@@ -277,77 +285,83 @@
 
     lax.fori_loop(0, 3, late, 0)
 
-    for u, slot in ((1, 7), (2, 8)):
+    for u, slot in ((1, 7), (2, 8), (0, 5), (0, 6)):
         unite(u, slot)
+    for u in (0, 1, 2):
         pack_rows(u)
-        send_rows(u)
     for h in (0, 1):
         arrived(held.at[3, half(h)], r_held.at[3, h])
     for b in (0, 1, 2):
         multiply(3, 1, b, 4 * b + 3)
     fold(3, [tile_of(3, b) for b in (0, 1, 2)])
-    pack_rows(3)
-    send_rows(3)
-    sub = lax.broadcasted_iota(jnp.int32, (2, BLK), 0)
-
-    def pack_columns(b, carry):
+    for n, b in ((0, 1), (1, 0), (2, 2)):
         m, l = col_m[b], col_l[b]
         top = jnp.max(m, axis=0, keepdims=True)
-        total = jnp.sum(l * jnp.exp2(m - top), axis=0, keepdims=True)
-        mp[b] = jnp.where(sub == 0, top, total)
-        return carry
-
-    lax.fori_loop(0, 3, pack_columns, 0)
-    for j in (0, 1):
+        mp[n, 0:1, :] = top
+        mp[n, 1:2, :] = jnp.sum(l * jnp.exp2(m - top), axis=0, keepdims=True)
+    for way in (0, 1):
         for g in (0, 1):
-            go(rcopy(mp.at[j + 1], mi.at[2 * j + t], s_mid.at[2 * j + g], r_mid.at[2 * j + t],
-                     at(g, (-1, 1)[j], 0)))
-    go(rcopy(mp.at[0], mi.at[4], s_mid.at[4], r_mid.at[4], mate))
-    for slot in (5, 6):
-        unite(0, slot)
-    pack_rows(0)
-    li[3] = jnp.where(sub[:, 0:HALF] == 0, NEG, 0.0)
+            go(rcopy(mp.at[way:way + 2], m1.at[way, t], s_mid.at[4 + 2 * way + g], r_mid.at[2 + 2 * way + t],
+                     at(g, 2 * way - 1, 0)))
+            go(rcopy(mp.at[2 * way], m2.at[way, t], s_mid.at[8 + 2 * way + g], r_mid.at[6 + 2 * way + t],
+                     at(g, 4 * way - 2, 0)))
+    go(rcopy(mp, m3, s_mid.at[12], r_mid.at[10], mate))
+    pack_rows(3)
+    for k in (2, 1, 3):
+        go(rcopy(lp.at[0:3], li.at[k - 1], s_mid.at[12 + k], r_mid.at[10 + k], at(t, 0, k)))
 
     def merge(parts):
-        tops = [p[0:1, :] for p in parts]
+        tops = [m for m, _ in parts]
         top = tops[0]
         for other in tops[1:]:
             top = jnp.maximum(top, other)
-        total = parts[0][1:2, :] * jnp.exp2(tops[0] - top)
+        total = parts[0][1] * jnp.exp2(tops[0] - top)
         for n in range(1, len(parts)):
-            total = total + parts[n][1:2, :] * jnp.exp2(tops[n] - top)
+            total = total + parts[n][1] * jnp.exp2(tops[n] - top)
         return top + jnp.log(total) * LOG2E
 
-    for n in range(5):
-        arrived(mi.at[n], r_mid.at[n])
-    mf[0] = merge([mp[0]] + [mi[n] for n in range(5)]) - jnp.log(wts[1][0:1, :]) * LOG2E
-    for j in (0, 1):
-        go(rcopy(mf.at[0], mf.at[j + 1], s_mid.at[9 + j], r_mid.at[9 + j], at(t, (1, -1)[j], 0)))
+    for way in (0, 1):
+        arrived(lx.at[way], r_mid.at[way])
+        for g in (0, 1):
+            arrived(m1.at[way, g], r_mid.at[2 + 2 * way + g])
+            arrived(m2.at[way, g], r_mid.at[6 + 2 * way + g])
+    arrived(m3, r_mid.at[10])
+
+    def pair(ref, *index):
+        return ref[index + (slice(0, 1),)], ref[index + (slice(1, 2),)]
+
+    both = (0, 1)
+    mf[0] = merge([pair(mp, 1), pair(m3, 1)] + [pair(m1, 0, g, 0) for g in both] + [pair(m1, 1, g, 1) for g in both]
+                  ) - mp[1, 2:3, :]
+    mf[1] = merge([pair(mp, 0), pair(m3, 0)] + [pair(m1, 1, g, 0) for g in both] + [pair(m2, 1, g) for g in both]
+                  ) - m1[1, 0, 0, 2:3, :]
+    mf[2] = merge([pair(mp, 2), pair(m3, 2)] + [pair(m1, 0, g, 1) for g in both] + [pair(m2, 0, g) for g in both]
+                  ) - m1[0, 0, 1, 2:3, :]
     for k in (1, 2, 3):
-        arrived(li.at[k - 1], r_mid.at[4 + k])
-
-    @pl.when(edge)
-    def _():
-        arrived(li.at[4], r_mid.at[8])
-        li[3] = li[4]
-
-    w_half = wts[0, :, pl.ds(pl.multiple_of(HALF * t, HALF), HALF)][0:1, :]
-    lf[0] = merge([lp[0]] + [li[n] for n in range(4)]) - jnp.log(w_half) * LOG2E
-    for k in (1, 2, 3):
-        go(rcopy(lf.at[0], lf.at[(4 - k) ^ ((4 - k) // 2)], s_mid.at[10 + k], r_mid.at[10 + 4 - k], at(t, 0, k)))
-
-    edge_go(rcopy(lf.at[0], lf.at[4], s_mid.at[14], r_mid.at[14], across))
-
-    for k in (1, 2, 3):
-        arrived(lf.at[k ^ (k // 2)], r_mid.at[10 + k])
-
-    def turn(k):
-        lcol[k] = jnp.broadcast_to(lf[k], (128, HALF)).T
-
-    for k in range(4):
-        turn(k)
-    for j in (0, 1):
-        arrived(mf.at[j + 1], r_mid.at[9 + j])
+        arrived(li.at[k - 1], r_mid.at[10 + k])
+
+    def line_of(ref, n):
+        return ref[0, n:n + 1, :], ref[1, n:n + 1, :]
+
+    def far_part(column):
+        m = jnp.where(column == 3, lx[0, 0:1, :], jnp.where(column == 0, lx[1, 0:1, :], NEG))
+        l = jnp.where(column == 3, lx[0, 1:2, :], jnp.where(column == 0, lx[1, 1:2, :], 0.0))
+        return m, l
+
+    for u in range(4):
+        k = u ^ (u // 2)
+        parts = [line_of(lp, u), far_part((y + k) % COLS)]
+        for other in (1, 2, 3):
+            theirs = (k - other) % 4
+            parts.append(line_of(li.at[3 - other], theirs ^ (theirs // 2)))
+        lf[u] = merge(parts) - (lp[2, 0:1, :] if k == 0 else li[3 - k, 2, 0:1, :])
+    edge_go(rcopy(lf.at[0], lf.at[4], s_mid.at[16], r_mid.at[14], across))
+
+    def turn(u):
+        lcol[u] = jnp.broadcast_to(lf[u], (128, HALF)).T
+
+    for u in range(4):
+        turn(u)
 
     def derive(slot, blocks, diagonal=False):
         cols = [jnp.broadcast_to(mf[b], (CH, BLK)) for b, _ in blocks]
@@ -398,20 +412,16 @@
             if rows is others:
                 go(rcopy(zf.at[b, others], zr.at[b], s_out.at[sem], r_out.at[sem], mate))
 
+    derive_units(0, 4, (late_b,))
+    col_grad(late_b, 5)
+    derive_units(3, 4, (0, edge_b))
+
     @pl.when(edge)
     def _():
         arrived(lf.at[4], r_mid.at[14])
         turn(4)
         derive(4, [(edge_b, 12)])
-
-    derive_units(0, 4, (late_b,))
-    col_grad(late_b, 5)
-
-    @pl.when(edge)
-    def _():
         xo[...] = jnp.dot(mass[12], video(edge_b), preferred_element_type=F32)
-
-    derive_units(3, 4, (0, edge_b))
 
     def send_lines(b, sem, base, down, order):
         arrived(zr.at[b], r_out.at[sem])
@@ -433,8 +443,8 @@
     col_grad(edge_b, 6, True)
     derive(0, [(0, 0)], True)
     derive_units(1, 3, (0,))
+    send_lines(edge_b, 6, 1, sgn, 1 - sel)
     yp[...] = row_grad(1, 2).reshape(2, HALF, D)
-    send_lines(edge_b, 6, 1, sgn, 1 - sel)
 
     for step in range(4):
         q = step + sel * (3 - 2 * step)
@@ -510,12 +520,15 @@
         pltpu.VMEM((9, HALF, 128), F32),
         pltpu.VMEM((3, 8, BLK), F32),
         pltpu.VMEM((3, 8, BLK), F32),
-        pltpu.VMEM((5, 2, HALF), F32),
-        pltpu.VMEM((5, 2, HALF), F32),
+        pltpu.VMEM((4, 4, HALF), F32),
+        pltpu.VMEM((3, 3, 4, HALF), F32),
+        pltpu.VMEM((2, 4, HALF), F32),
         pltpu.VMEM((5, 1, HALF), F32),
         pltpu.VMEM((5, HALF, 128), F32),
-        pltpu.VMEM((3, 2, BLK), F32),
-        pltpu.VMEM((5, 2, BLK), F32),
+        pltpu.VMEM((3, 4, BLK), F32),
+        pltpu.VMEM((2, 2, 2, 4, BLK), F32),
+        pltpu.VMEM((2, 2, 4, BLK), F32),
+        pltpu.VMEM((3, 4, BLK), F32),
         pltpu.VMEM((3, 1, BLK), F32),
         pltpu.VMEM((HALF, D), F32),
         pltpu.VMEM((2, HALF, D), F32),
@@ -530,7 +543,7 @@
         pltpu.VMEM((2, HALF, D), BF16),
         pltpu.VMEM((2, HALF, D), BF16),
         pltpu.VMEM((2, HALF, D), F32),
-        dma((21,)), dma((1,)), dma((16,)), dma((UNITS, 4)), dma((15,)), dma((15,)), dma((14,)), dma((14,)),
+        dma((21,)), dma((1,)), dma((16,)), dma((UNITS, 4)), dma((17,)), dma((15,)), dma((14,)), dma((14,)),
         dma((2, 4)), dma((2, 4)), dma((2, 4)), dma((2, 4)), dma((4,)), dma((4,)), dma((4,)),
     ]
     return pl.pallas_call(

time: 78.8 us -> 74.9 us (0.951)
  Pallas kernels: 75.4 us -> 71.6 us
    pallas_call x1, Pallas kernels: 75.4 us -> 71.6 us  [on_device(): pl.pallas_call(kernel, out_shape=jax.ShapeDtypeStruct((1, BLK, D), F32),...]
where the time goes in v4:
time: 74.9 us; the launch traced here: 74.8 us
  Pallas kernels  71.6 us (96%)
  local copies, waits for them, and re-layouts  3.16 us (4%)
    pallas_call x1, Pallas kernels, on_device(): pl.pallas_call(kernel, out_shape=jax.ShapeDtypeStruct((1, BLK, D), F32),...  71.6 us
    unnamed x1, local copies, waits for them, and re-layouts  3.16 us

profile of v4, /device:TPU:1, one launch (start us, length us, event | category | flops | bytes accessed | tf_op | source)
XLA Modules:
  0.0 74.8 jit_solution(16314587205379402939)
XLA Ops:
  0.0 71.6 %shard_map.46 = f32[1,512,1024]{2,1,0:T(8,128)} custom-call(s32[128]{0:T(128)} %ds_ref.1, f32[42]{0:T(128)} %scale_ref.1, bf16[1,512,1024]{2,1,0:T(8,128)(2,1)} %x_ref.1, bf16[1,512]{1,0:T(2,128)(2,1)} %wt_ref.1), custom_call_target="tpu_custom_call" | custom-call | tf_op jit(solution)/shard_map/pallas_call | solution.py:549
  71.7 3.2 %copy.6 = f32[1,512,1024]{2,1,0:T(8,128)} copy(f32[1,512,1024]{2,1,0:T(8,128)} %shard_map.46) | data formatting | bytes 4194304

commit v5 on v4

--- a/solution.py
+++ b/solution.py
@@ -19,8 +19,8 @@
 
 
 def kernel(ds_ref, scale_ref, x_ref, wt_ref, out_ref, held, score, mass, wts,
-           row_m, row_l, col_m, col_l, lp, li, lx, lf, lcol, mp, m1, m2, m3, mf,
-           ya, yp, yo, yi, yt, yr, xs, xo, zf, zr, zo, zi, ends,
+           row_m, row_l, col_m, col_l, lp, li, lx, lq, lf, lcol, mp, m1, m2, m3, mf,
+           ya, yp, yo, yi, yt, yr, xs, zf, zr, zo, zi, ends,
            s_in, r_in, s_held, r_held, s_mid, r_mid, s_out, r_out, s_y, r_y, s_z, r_z, s_home, s_away, r_away):
     t = lax.axis_index("tower")
     tile = lax.axis_index("tile")
@@ -41,7 +41,6 @@
             src_ref=src, dst_ref=dst, send_sem=ss, recv_sem=rs, device_id=dev, device_id_type=MESH)
 
     mate = at(1 - t, 0, 0)
-    across = at(t, -sgn, edge_k)
 
     def arrived(ref, sem):
         rcopy(ref, ref, sem, sem, mate).wait_recv()
@@ -276,8 +275,12 @@
 
     for c in range(COLS):
         edge_go(rcopy(lp.at[3], lx.at[sel], s_mid.at[c], r_mid.at[sel], at(t, -sgn, c)))
+    for h in (0, 1):
+        arrived(held.at[3, half(h)], r_held.at[3, h])
+    multiply(3, 1, 0, 3)
+    multiply(3, 1, edge_b, 4 * edge_b + 3)
     shared(late_b)
-    multiply(0, 3, late_b, 4 * late_b)
+    multiply(0, 4, late_b, 4 * late_b)
 
     def late(u, carry):
         fold(6 + u, [tile_of(u, late_b)])
@@ -285,14 +288,6 @@
 
     lax.fori_loop(0, 3, late, 0)
 
-    for u, slot in ((1, 7), (2, 8), (0, 5), (0, 6)):
-        unite(u, slot)
-    for u in (0, 1, 2):
-        pack_rows(u)
-    for h in (0, 1):
-        arrived(held.at[3, half(h)], r_held.at[3, h])
-    for b in (0, 1, 2):
-        multiply(3, 1, b, 4 * b + 3)
     fold(3, [tile_of(3, b) for b in (0, 1, 2)])
     for n, b in ((0, 1), (1, 0), (2, 2)):
         m, l = col_m[b], col_l[b]
@@ -306,7 +301,12 @@
             go(rcopy(mp.at[2 * way], m2.at[way, t], s_mid.at[8 + 2 * way + g], r_mid.at[6 + 2 * way + t],
                      at(g, 4 * way - 2, 0)))
     go(rcopy(mp, m3, s_mid.at[12], r_mid.at[10], mate))
-    pack_rows(3)
+    for u, slot in ((1, 7), (2, 8), (0, 5), (0, 6)):
+        unite(u, slot)
+    for u in range(4):
+        pack_rows(u)
+    go(rcopy(lp.at[0:3], lq.at[y], s_mid.at[16], r_mid.at[14 + y], at(t, 1, COLS - y)))
+    go(rcopy(lp.at[0:3], lq.at[y], s_mid.at[17], r_mid.at[14 + y], at(t, -1, COLS - 1 - y)))
     for k in (2, 1, 3):
         go(rcopy(lp.at[0:3], li.at[k - 1], s_mid.at[12 + k], r_mid.at[10 + k], at(t, 0, k)))
 
@@ -355,13 +355,22 @@
             theirs = (k - other) % 4
             parts.append(line_of(li.at[3 - other], theirs ^ (theirs // 2)))
         lf[u] = merge(parts) - (lp[2, 0:1, :] if k == 0 else li[3 - k, 2, 0:1, :])
-    edge_go(rcopy(lf.at[0], lf.at[4], s_mid.at[16], r_mid.at[14], across))
 
     def turn(u):
         lcol[u] = jnp.broadcast_to(lf[u], (128, HALF)).T
 
     for u in range(4):
         turn(u)
+
+    def turn_far():
+        parts = [(lp[3, 0:1, :], lp[3, 1:2, :])]
+        for c in range(COLS):
+            arrived(lq.at[c], r_mid.at[14 + c])
+            one, two = (k ^ (k // 2) for k in ((3 - c) % 4, (0 - c) % 4))
+            parts.append(tuple(jnp.where(sel == 0, lq[c, n, one:one + 1, :], lq[c, n, two:two + 1, :])
+                               for n in (0, 1)))
+        lf[4] = merge(parts) - jnp.where(sel == 0, lq[3, 2, 0:1, :], lq[0, 2, 0:1, :])
+        turn(4)
 
     def derive(slot, blocks, diagonal=False):
         cols = [jnp.broadcast_to(mf[b], (CH, BLK)) for b, _ in blocks]
@@ -399,52 +408,63 @@
     mine = pl.ds(pl.multiple_of(HALF * t, HALF), HALF)
     others = pl.ds(pl.multiple_of(HALF * (1 - t), HALF), HALF)
 
-    def col_grad(b, sem, far=False):
-        for rows in (others, mine):
-            g = mass[pl.ds(4 * b, 4), :, rows].reshape(4 * HALF, HALF)
-            a = held[0:4].reshape(4 * HALF, D)
-            zf[b, rows] = lax.dot_general(g, a, (((0,), (0,)), ((), ())), preferred_element_type=F32)
-            if far:
-                @pl.when(edge)
-                def _():
-                    zf[b, rows] += lax.dot_general(mass[12, :, rows], held[4 + 2 * late_b + t],
-                                                   (((0,), (0,)), ((), ())), preferred_element_type=F32)
-            if rows is others:
-                go(rcopy(zf.at[b, others], zr.at[b], s_out.at[sem], r_out.at[sem], mate))
-
-    derive_units(0, 4, (late_b,))
-    col_grad(late_b, 5)
-    derive_units(3, 4, (0, edge_b))
-
-    @pl.when(edge)
-    def _():
-        arrived(lf.at[4], r_mid.at[14])
-        turn(4)
-        derive(4, [(edge_b, 12)])
-        xo[...] = jnp.dot(mass[12], video(edge_b), preferred_element_type=F32)
+    def col_grad(b, rows, far=False):
+        g = mass[pl.ds(4 * b, 4), :, rows].reshape(4 * HALF, HALF)
+        a = held[0:4].reshape(4 * HALF, D)
+        zf[b, rows] = lax.dot_general(g, a, (((0,), (0,)), ((), ())), preferred_element_type=F32)
+        if far:
+            @pl.when(edge)
+            def _():
+                zf[b, rows] += lax.dot_general(mass[12, :, rows], held[4 + 2 * late_b + t],
+                                               (((0,), (0,)), ((), ())), preferred_element_type=F32)
+
+    def hand_over(b, sem):
+        go(rcopy(zf.at[b, others], zr.at[b], s_out.at[sem], r_out.at[sem], mate))
 
     def send_lines(b, sem, base, down, order):
         arrived(zr.at[b], r_out.at[sem])
-        zo[b - 1] = (zf[b, mine] + zr[b]).astype(BF16)
         for step in range(4):
             q = step + order * (3 - 2 * step)
+            mine_q = pl.ds(pl.multiple_of(HALF * t + PART * q, PART), PART)
+            zo[b - 1, part(q)] = (zf[b, mine_q] + zr[b, part(q)]).astype(BF16)
             go(rcopy(zo.at[b - 1, part(q)], zi.at[b - 1, part(q)], s_z.at[base, q], r_z.at[b - 1, q],
                      at(t, down, 0)))
 
-    @pl.when(edge)
-    def _():
-        zf[late_b, mine] += xo[...]
-
-    send_lines(late_b, 5, 0, -sgn, sel)
+    derive_units(0, 4, (late_b,))
+    col_grad(late_b, others)
+    hand_over(late_b, 5)
+    derive_units(3, 4, (0, edge_b))
     yt[...] = row_grad(3, 1).astype(BF16)
     for h, way in ((0, 1), (1, -1)):
         go(rcopy(yt.at[half(h)], yr.at[h], s_out.at[2 + h], r_out.at[2 + h], at(t, 0, way)))
+    col_grad(late_b, mine)
+
+    @pl.when(edge)
+    def _():
+        turn_far()
+        derive(4, [(edge_b, 12)])
+        zf[late_b, mine] += jnp.dot(mass[12], video(edge_b), preferred_element_type=F32)
+
+    send_lines(late_b, 5, 0, -sgn, sel)
     derive_units(0, 3, (edge_b,))
-    col_grad(edge_b, 6, True)
+    col_grad(edge_b, others, True)
+    hand_over(edge_b, 6)
     derive(0, [(0, 0)], True)
     derive_units(1, 3, (0,))
+    yp[...] = row_grad(1, 2).reshape(2, HALF, D)
+    early_parts = {}
+    for step in (0, 1):
+        for n, q in ((0, 3 - step), (1, step)):
+            copy = rcopy(yo.at[n, part(q)], yi.at[n, part(q)], s_y.at[n, q], r_y.at[n, q], at(t, 0, 1 - 2 * n))
+            early_parts[n, q] = copy
+            pending.append(copy)
+
+            @pl.when(jnp.logical_not(edge & (sel == 1 - n)))
+            def _():
+                yo[n, part(q)] = yp[n, part(q)].astype(BF16)
+                copy.start()
+    col_grad(edge_b, mine, True)
     send_lines(edge_b, 6, 1, sgn, 1 - sel)
-    yp[...] = row_grad(1, 2).reshape(2, HALF, D)
 
     for step in range(4):
         q = step + sel * (3 - 2 * step)
@@ -459,10 +479,18 @@
                 arrived(yr.at[n], r_out.at[2 + n])
                 yp[n, half(n)] += yr[n].astype(F32)
         for n, q in ((0, 3 - step), (1, step)):
-            yo[n, part(q)] = yp[n, part(q)].astype(BF16)
-            go(rcopy(yo.at[n, part(q)], yi.at[n, part(q)], s_y.at[n, q], r_y.at[n, q], at(t, 0, 1 - 2 * n)))
-
-    col_grad(0, 4)
+            if step < 2:
+                @pl.when(edge & (sel == 1 - n))
+                def _():
+                    yo[n, part(q)] = yp[n, part(q)].astype(BF16)
+                    early_parts[n, q].start()
+            else:
+                yo[n, part(q)] = yp[n, part(q)].astype(BF16)
+                go(rcopy(yo.at[n, part(q)], yi.at[n, part(q)], s_y.at[n, q], r_y.at[n, q], at(t, 0, 1 - 2 * n)))
+
+    col_grad(0, others)
+    hand_over(0, 4)
+    col_grad(0, mine)
     ya[...] = row_grad(0, 1)
 
     temper = scale_ref[block_of(0, 0)]
@@ -523,6 +551,7 @@
         pltpu.VMEM((4, 4, HALF), F32),
         pltpu.VMEM((3, 3, 4, HALF), F32),
         pltpu.VMEM((2, 4, HALF), F32),
+        pltpu.VMEM((4, 3, 4, HALF), F32),
         pltpu.VMEM((5, 1, HALF), F32),
         pltpu.VMEM((5, HALF, 128), F32),
         pltpu.VMEM((3, 4, BLK), F32),
@@ -537,13 +566,12 @@
         pltpu.VMEM((HALF, D), BF16),
         pltpu.VMEM((2, HALF // 2, D), BF16),
         pltpu.VMEM((HALF, D), BF16),
-        pltpu.VMEM((HALF, D), F32),
         pltpu.VMEM((3, BLK, D), F32),
         pltpu.VMEM((3, HALF, D), F32),
         pltpu.VMEM((2, HALF, D), BF16),
         pltpu.VMEM((2, HALF, D), BF16),
         pltpu.VMEM((2, HALF, D), F32),
-        dma((21,)), dma((1,)), dma((16,)), dma((UNITS, 4)), dma((17,)), dma((15,)), dma((14,)), dma((14,)),
+        dma((21,)), dma((1,)), dma((16,)), dma((UNITS, 4)), dma((18,)), dma((18,)), dma((14,)), dma((14,)),
         dma((2, 4)), dma((2, 4)), dma((2, 4)), dma((2, 4)), dma((4,)), dma((4,)), dma((4,)),
     ]
     return pl.pallas_call(

time: 74.9 us -> 74.2 us (level)
  no operation moved by 1% of the time
where the time goes in v5:
time: 74.2 us; the launch traced here: 74.1 us
  Pallas kernels  70.9 us (96%)
  local copies, waits for them, and re-layouts  3.16 us (4%)
    pallas_call x1, Pallas kernels, on_device(): pl.pallas_call(kernel, out_shape=jax.ShapeDtypeStruct((1, BLK, D), F32),...  70.9 us
    unnamed x1, local copies, waits for them, and re-layouts  3.16 us

profile of v5, /device:TPU:1, one launch (start us, length us, event | category | flops | bytes accessed | tf_op | source)
XLA Modules:
  0.0 74.1 jit_solution(10791412900849967471)
XLA Ops:
  0.0 70.9 %shard_map.46 = f32[1,512,1024]{2,1,0:T(8,128)} custom-call(s32[128]{0:T(128)} %ds_ref.1, f32[42]{0:T(128)} %scale_ref.1, bf16[1,512,1024]{2,1,0:T(8,128)(2,1)} %x_ref.1, bf16[1,512]{1,0:T(2,128)(2,1)} %wt_ref.1), custom_call_target="tpu_custom_call" | custom-call | tf_op jit(solution)/shard_map/pallas_call | solution.py:577
  70.9 3.2 %copy.6 = f32[1,512,1024]{2,1,0:T(8,128)} copy(f32[1,512,1024]{2,1,0:T(8,128)} %shard_map.46) | data formatting | bytes 4194304

commit v6 on v5

--- a/solution.py
+++ b/solution.py
@@ -148,14 +148,15 @@
             preferred_element_type=F32).reshape(count, HALF, BLK)
 
     def fold(slot, blocks):
+        ch = 2 * CH if len(blocks) < 3 else CH
         def rows(c, tops):
-            at_rows = pl.ds(pl.multiple_of(c * CH, CH), CH)
+            at_rows = pl.ds(pl.multiple_of(c * ch, ch), ch)
             parts, peaks = [], []
             for n, (b, index, mult, off) in enumerate(blocks):
                 s = score[index, at_rows, :] * mult + off
                 score[index, at_rows, :] = s
                 peak = tops[n]
-                for e in range(0, CH, 8):
+                for e in range(0, ch, 8):
                     peak = jnp.maximum(peak, s[e:e + 8])
                 peaks.append(peak)
                 parts.extend([s[:, 128 * q:128 * q + 128] for q in range(4)])
@@ -170,21 +171,21 @@
             return tuple(peaks)
 
         old = [col_m[b] for b, _, _, _ in blocks]
-        new = lax.fori_loop(0, HALF // CH, rows, tuple(old))
+        new = lax.fori_loop(0, HALF // ch, rows, tuple(old))
 
         def columns(c, sums):
-            at_rows = pl.ds(pl.multiple_of(c * CH, CH), CH)
+            at_rows = pl.ds(pl.multiple_of(c * ch, ch), ch)
             result = []
             for n, (b, index, mult, off) in enumerate(blocks):
                 s = score[index, at_rows, :]
                 total = sums[n]
-                for e in range(0, CH, 8):
+                for e in range(0, ch, 8):
                     total = total + jnp.exp2(s[e:e + 8] - new[n])
                 result.append(total)
             return tuple(result)
 
         begin = tuple(col_l[b] * jnp.exp2(old[n] - new[n]) for n, (b, _, _, _) in enumerate(blocks))
-        sums = lax.fori_loop(0, HALF // CH, columns, begin)
+        sums = lax.fori_loop(0, HALF // ch, columns, begin)
         for n, (b, _, _, _) in enumerate(blocks):
             col_m[b] = new[n]
             col_l[b] = sums[n]
@@ -373,23 +374,24 @@
         turn(4)
 
     def derive(slot, blocks, diagonal=False):
-        cols = [jnp.broadcast_to(mf[b], (CH, BLK)) for b, _ in blocks]
+        ch = 2 * CH if len(blocks) < 3 else CH
+        cols = [jnp.broadcast_to(mf[b], (ch, BLK)) for b, _ in blocks]
 
         def rows(c, carry):
-            at_rows = pl.ds(pl.multiple_of(c * CH, CH), CH)
+            at_rows = pl.ds(pl.multiple_of(c * ch, ch), ch)
             lse = jnp.concatenate([lcol[slot, at_rows, :]] * 4, axis=1)
             for n, (b, index) in enumerate(blocks):
                 s = score[index, at_rows, :]
                 g = jnp.exp2(s - lse) + jnp.exp2(s - cols[n])
                 if diagonal:
-                    r_id = lax.broadcasted_iota(jnp.int32, (CH, BLK), 0) + c * CH + HALF * t
-                    c_id = lax.broadcasted_iota(jnp.int32, (CH, BLK), 1)
-                    both = jnp.broadcast_to(wts[0][0:1, :] + wts[1][0:1, :], (CH, BLK))
+                    r_id = lax.broadcasted_iota(jnp.int32, (ch, BLK), 0) + c * ch + HALF * t
+                    c_id = lax.broadcasted_iota(jnp.int32, (ch, BLK), 1)
+                    both = jnp.broadcast_to(wts[0][0:1, :] + wts[1][0:1, :], (ch, BLK))
                     g = g - jnp.where(r_id == c_id, both, 0.0)
                 mass[index, at_rows, :] = g.astype(BF16)
             return carry
 
-        lax.fori_loop(0, HALF // CH, rows, 0)
+        lax.fori_loop(0, HALF // ch, rows, 0)
 
     def derive_units(first, last, blocks):
         def one(u, carry):

time: 74.2 us -> 73.8 us (level)
  no operation moved by 1% of the time
where the time goes in v6:
time: 73.8 us; the launch traced here: 73.7 us
  Pallas kernels  70.5 us (96%)
  local copies, waits for them, and re-layouts  3.16 us (4%)
    pallas_call x1, Pallas kernels, on_device(): pl.pallas_call(kernel, out_shape=jax.ShapeDtypeStruct((1, BLK, D), F32),...  70.5 us
    unnamed x1, local copies, waits for them, and re-layouts  3.16 us

profile of v6, /device:TPU:1, one launch (start us, length us, event | category | flops | bytes accessed | tf_op | source)
XLA Modules:
  0.0 73.7 jit_solution(5137427630299018991)
XLA Ops:
  0.0 70.5 %shard_map.46 = f32[1,512,1024]{2,1,0:T(8,128)} custom-call(s32[128]{0:T(128)} %ds_ref.1, f32[42]{0:T(128)} %scale_ref.1, bf16[1,512,1024]{2,1,0:T(8,128)(2,1)} %x_ref.1, bf16[1,512]{1,0:T(2,128)(2,1)} %wt_ref.1), custom_call_target="tpu_custom_call" | custom-call | tf_op jit(solution)/shard_map/pallas_call | solution.py:579
  70.5 3.2 %copy.6 = f32[1,512,1024]{2,1,0:T(8,128)} copy(f32[1,512,1024]{2,1,0:T(8,128)} %shard_map.46) | data formatting | bytes 4194304
